TPU v7x, 128 devices: a whole 4x4x4 slice. The times are simulated.
128 devices in a mesh: sx: 16 (over x, y), sy: 8 (over z, core).
Axes of the slice: x: 4, y: 4, z: 4, core: 2. Of those that a mesh axis runs over, the one named last changes fastest.
Arguments:
- panels: bfloat16 [128, 384, 400], P(('sx', 'sy')), may hold values from -0.3125 to 0.3125
- coupling: bfloat16 [1024, 2, 384, 384], P(('sx', 'sy')), may hold values from -6 to 6
- partner: int32 [1024], P(('sx', 'sy')), may hold values from 0 to 23, as said below
- counts: int32 [1024], P(('sx', 'sy')), may hold values from 48 to 384
Outputs:
- pair_blocks: bfloat16 [1024, 2, 400, 400], P(('sx', 'sy'))
- partner_blocks: float32 [128, 2, 400, 400], P(('sx', 'sy'))
Inputs may be any that keep to these rules, and one draw needn't show every extreme that they name: `partner`: A code below 16 names the substructure with that sx index in the first substructure's sy column; a code c of 16 or more names the one with sy index c - 16 in its sx row; a pair never names its own first substructure.
All inputs are finite; a program needn't handle non-finite values.
Results may differ from a plain program's by a relative error of at most 0.014.
Values may be sent and summed in bfloat16 or wider, within the bound.
No kernel may reach another device: no remote copies, remote signals or barrier semaphores. Data moves between devices by JAX's collectives and lax.ppermute only.
A program may use at most 192 MiB of HBM per device.

v0:
```python
import jax
import jax.numpy as jnp
from jax import lax
from jax.sharding import PartitionSpec as P


def padded_product(own, coupling, counts):
    width = coupling.shape[2]
    rowpos = jnp.arange(width, dtype=jnp.int32)
    keep = (rowpos[None, :, None] < counts[:, None, None]) & (
        rowpos[None, None, :] < counts[:, None, None]
    )
    masked = jnp.where(keep[:, None], coupling, jnp.zeros_like(coupling))
    return jnp.einsum("bm,ptbk->ptmk", own, masked, preferred_element_type=jnp.float32).astype(
        jnp.bfloat16
    )


def body(panels, coupling, partner, counts):
    span_x = lax.axis_size("sx")
    own = panels[0]
    along_x = partner < span_x
    code_y = partner - span_x
    left_product = padded_product(own, coupling, counts)
    piece = lax.all_gather(panels, "sx", axis=0, tiled=True)
    slots = jnp.arange(piece.shape[0], dtype=jnp.int32)
    hit = (along_x[:, None] & (partner[:, None] == slots[None, :])).astype(jnp.bfloat16)
    from_rows = jnp.einsum("pk,kbm->pbm", hit, piece, preferred_element_type=jnp.float32)
    piece = lax.all_gather(panels, "sy", axis=0, tiled=True)
    slots = jnp.arange(piece.shape[0], dtype=jnp.int32)
    hit = ((~along_x)[:, None] & (code_y[:, None] == slots[None, :])).astype(jnp.bfloat16)
    from_cols = jnp.einsum("pk,kbm->pbm", hit, piece, preferred_element_type=jnp.float32)
    right_panels = (from_rows + from_cols).astype(jnp.bfloat16)
    full = jnp.einsum(
        "ptmb,pbn->ptmn", left_product, right_panels, preferred_element_type=jnp.float32
    )
    pair_blocks = full.astype(jnp.bfloat16)
    slots = jnp.arange(1 * lax.axis_size("sx"), dtype=jnp.int32)
    gathered_rows = lax.psum_scatter(
        jnp.einsum(
            "pk,ptmn->ktnm",
            (along_x[:, None] & (partner[:, None] == slots[None, :])).astype(jnp.float32),
            full,
            precision=lax.Precision.HIGHEST,
        ).astype(jnp.bfloat16),
        "sx",
        scatter_dimension=0,
        tiled=True,
    ).astype(jnp.float32)
    slots = jnp.arange(1 * lax.axis_size("sy"), dtype=jnp.int32)
    gathered_cols = lax.psum_scatter(
        jnp.einsum(
            "pk,ptmn->ktnm",
            ((~along_x)[:, None] & (code_y[:, None] == slots[None, :])).astype(jnp.float32),
            full,
            precision=lax.Precision.HIGHEST,
        ).astype(jnp.bfloat16),
        "sy",
        scatter_dimension=0,
        tiled=True,
    ).astype(jnp.float32)
    partner_blocks = gathered_rows + gathered_cols
    return (pair_blocks, partner_blocks)


def solution(mesh):
    placed = (
        P(("sx", "sy"), None, None),
        P(("sx", "sy"), None, None, None),
        P(("sx", "sy")),
        P(("sx", "sy")),
    )
    return jax.shard_map(
        body,
        mesh=mesh,
        in_specs=placed,
        out_specs=(P(("sx", "sy"), None, None, None), P(("sx", "sy"), None, None, None)),
        check_vma=False,
    )
```

profile of v0, /device:TPU:0, one launch (start us, length us, event | category | flops | bytes accessed | tf_op | source)
XLA Modules:
  0.0 307.0 jit_solution(11047373944037555037)
XLA Ops:
  7.2 0.0 copy-start.1
  7.2 0.0 all-gather.5.cloned.1.call-start
  7.2 0.7 all-gather.5.cloned.1.call-update
  7.9 0.0 all-gather.3.cloned.1.call-start
  8.0 0.7 all-gather.3.cloned.1.call-update
  8.7 0.0 reduce-scatter.5.cloned.1.call-start
  8.7 0.7 broadcast_add_fusion
  9.4 0.7 broadcast_compare_fusion
  10.0 0.7 iota_compare_fusion
  10.8 0.7 broadcast_and_fusion
  11.4 26.8 %all-gather.5.cloned.1.call-done = bf16[8,384,400]{1,2,0:T(8,128)(2,1)} async-done(((bf16[1,384,400]{1,2,0:T(8,128)(2,1)}), bf16[8,384,400]{1,2,0:T(8,128)(2,1)}) %all-gather.5.cloned.1.call-update) | async-done | bytes 2457616 | tf_op jit(solution)/shard_map/all_gather | solution.py:29
  38.2 5.1 %fusion.23 = f32[8,384,400]{1,0,2:T(8,128)} fusion(bf16[8,384,400]{1,2,0:T(8,128)(2,1)} %all-gather.5.cloned.1.call-done, s32[8]{0:T(128)S(1)} %broadcast_add_fusion, pred[8]{0:T(512)(128)(4,1)S(1)} %get-tuple-element.5), kind=kOutput, calls=%fused_computation.17 | convolution fusion | flops 19660928 | bytes 7372840 | tf_op jit(solution)/shard_map/pk,kbm->pbm/dot_general | solution.py:32
  43.4 52.2 %all-gather.3.cloned.1.call-done = bf16[16,384,400]{1,2,0:T(8,128)(2,1)} async-done(((bf16[1,384,400]{1,2,0:T(8,128)(2,1)}), bf16[16,384,400]{1,2,0:T(8,128)(2,1)}) %all-gather.3.cloned.1.call-update) | async-done | bytes 4915216 | tf_op jit(solution)/shard_map/all_gather | solution.py:25
  95.6 0.0 copy-done.1
  95.6 0.0 copy-start
  95.6 5.6 %fusion.9 = f32[8,384,400]{1,0,2:T(8,128)} fusion(bf16[16,384,400]{1,2,0:T(8,128)(2,1)} %all-gather.3.cloned.1.call-done, s32[8]{0:T(128)S(1)} %copy-done.1, pred[8]{0:T(512)(128)(4,1)S(1)} %get-tuple-element.4), kind=kOutput, calls=%fused_computation.10 | convolution fusion | flops 39321856 | bytes 9830440 | tf_op jit(solution)/shard_map/pk,kbm->pbm/dot_general | solution.py:28
  101.3 0.0 copy-done
  101.3 17.9 %fusion.50 = (bf16[8,2,400,400]{3,2,1,0:T(8,128)(2,1)}, f32[8,2,400,400]{3,2,1,0:T(8,128)}) fusion(f32[8,384,400]{1,0,2:T(8,128)} %fusion.23, f32[8,384,400]{1,0,2:T(8,128)} %fusion.9, bf16[8,2,384,384]{3,2,1,0:T(8,128)(2,1)} %param.5, pred[8,384,384]{2,1,0:T(8,128)(4,1)S(1)} %broadcast_and_fusion, bf16[1,384,400]{1,2,0:T(8,128)(2,1)S(1)} %copy-done), kind=kOutput, calls=%fused_computation.44 | convolution fusion | flops 3863351296 | bytes 31395840 | tf_op jit(solution)/shard_map/ptmb,pbn->ptmn/dot_general | solution.py:34
  119.2 19.4 %convert_bitcast_fusion = bf16[8,2,400,400]{2,0,3,1:T(8,128)(2,1)} fusion(f32[8,2,400,400]{3,2,1,0:T(8,128)} %get-tuple-element.7, s32[8]{0:T(128)S(1)} %broadcast_add_fusion, pred[8]{0:T(512)(128)(4,1)S(1)} %get-tuple-element.5), kind=kOutput, calls=%fused_computation.5 | convolution fusion | flops 248320128 | bytes 15360040 | tf_op jit(solution)/shard_map/pk,ptmn->ktnm/dot_general | solution.py:52
  138.6 13.3 %copy.12 = bf16[8,2,400,400]{3,2,1,0:T(8,128)(2,1)} copy(bf16[8,2,400,400]{2,0,3,1:T(8,128)(2,1)} %convert_bitcast_fusion) | data formatting | bytes 10240000 | tf_op jit(solution)/shard_map/convert_element_type | solution.py:57
  151.9 0.0 reduce-scatter.5.cloned.1.call-update
  151.9 0.0 reduce-scatter.7.cloned.1.call-start
  151.9 24.3 %fusion.3 = bf16[16,2,400,400]{2,0,3,1:T(8,128)(2,1)} fusion(f32[8,2,400,400]{3,2,1,0:T(8,128)} %get-tuple-element.7, s32[8]{0:T(128)S(1)} %copy-done.1, pred[8]{0:T(512)(128)(4,1)S(1)} %get-tuple-element.4), kind=kOutput, calls=%fused_computation.4 | convolution fusion | flops 496640256 | bytes 20480040 | tf_op jit(solution)/shard_map/pk,ptmn->ktnm/dot_general | solution.py:40
  176.3 25.6 %copy.10 = bf16[16,2,400,400]{3,2,1,0:T(8,128)(2,1)} copy(bf16[16,2,400,400]{2,0,3,1:T(8,128)(2,1)} %fusion.3) | data formatting | bytes 20480000 | tf_op jit(solution)/shard_map/convert_element_type | solution.py:45
  201.9 0.0 reduce-scatter.7.cloned.1.call-update
  201.9 0.0 reduce-scatter.5.cloned.1.call-done
  201.9 95.7 %reduce-scatter.7.cloned.1.call-done = bf16[1,2,400,400]{3,2,1,0:T(8,128)(2,1)} async-done(((bf16[16,2,400,400]{3,2,1,0:T(8,128)(2,1)}), bf16[1,2,400,400]{3,2,1,0:T(8,128)(2,1)}) %reduce-scatter.7.cloned.1.call-update) | async-done | bytes 640016
  297.6 2.8 convert_add_fusion
Async XLA Ops:
  7.2 88.4 %copy-start.1 = (s32[8]{0:T(128)S(1)}, s32[8]{0:T(128)}, u32[]{:S(2)}) copy-start(s32[8]{0:T(128)} %param.6) | copy-start | bytes 100
  7.2 31.0 %all-gather.5.cloned.1.call-start = ((), (), s32[]{:S(2)}) async-start(), calls=%async_computation.3 | async-start | bytes 2764800 | tf_op jit(solution)/shard_map/all_gather | solution.py:29
  7.9 87.7 %all-gather.3.cloned.1.call-start = ((), (), s32[]{:S(2)}) async-start(), calls=%async_computation.2 | async-start | bytes 5222400 | tf_op jit(solution)/shard_map/all_gather | solution.py:25
  8.7 193.2 %reduce-scatter.5.cloned.1.call-start = ((), (), s32[]{:S(2)}) async-start(), calls=%async_computation.4 | async-start | bytes 7372800 | tf_op jit(solution)/shard_map/reduce_scatter | solution.py:51
  95.6 5.7 %copy-start = (bf16[1,384,400]{1,2,0:T(8,128)(2,1)S(1)}, bf16[1,384,400]{1,2,0:T(8,128)(2,1)}, u32[]{:S(2)}) copy-start(bf16[1,384,400]{1,2,0:T(8,128)(2,1)} %param.4) | copy-start | bytes 921604
  151.9 145.7 %reduce-scatter.7.cloned.1.call-start = ((), (), s32[]{:S(2)}) async-start(), calls=%async_computation.5 | async-start | bytes 13926400
Sparse Core Ops, SparseCore 0:
  9.7 28.4 all-gather.4
  40.4 55.1 all-gather.2
  152.0 43.6 reduce-scatter.4
  202.0 95.5 reduce-scatter.6
where the time goes:
time: 309 us; the launch traced here: 307 us
  waiting for transfers between devices  176 us (57%)
  matrix products  72.4 us (23%)
  local copies, waits for them, and re-layouts  38.9 us (13%)
  between operations  13.8 us (4%)
  other arithmetic  5.55 us (2%)
    unnamed x5, waiting for transfers between devices  97.1 us
    all_gather x1, waiting for transfers between devices, body(): piece = lax.all_gather(panels, 'sx', axis=0, tiled=True)  52.2 us
    all_gather x1, waiting for transfers between devices, body(): piece = lax.all_gather(panels, 'sy', axis=0, tiled=True)  26.8 us
    convert_element_type x1, local copies, waits for them, and re-layouts, body(): gathered_rows = lax.psum_scatter(jnp.einsum('pk,ptmn->ktnm', (along_x[:,...  25.6 us
    dot_general x1, matrix products, body(): jnp.einsum('pk,ptmn->ktnm', (along_x[:, None] & (partner[:, None] == slot...  24.3 us
    dot_general x1, matrix products, body(): jnp.einsum('pk,ptmn->ktnm', ((~along_x)[:, None] & (code_y[:, None] == sl...  19.4 us
    dot_general x1, matrix products, body(): jnp.einsum('ptmb,pbn->ptmn', left_product, right_panels, preferred_elemen...  17.9 us
    convert_element_type x1, local copies, waits for them, and re-layouts, body(): gathered_cols = lax.psum_scatter(jnp.einsum('pk,ptmn->ktnm', ((~along_x)[...  13.3 us
  transfers between devices with their start and end apart: 4, of which 3 were waited for; matrix products, arithmetic and copies ran while one was open for 19% of the time, Pallas kernels for 0%

commit v1 on v0

v1 whole, which is shorter than its diff:
```python
import functools

import jax
import jax.numpy as jnp
from jax import lax
from jax.experimental import pallas as pl
from jax.experimental.pallas import tpu as pltpu
from jax.sharding import PartitionSpec as P


def left_kernel(along_ref, slot_ref, first_ref, used_x_ref, used_y_ref, counts_ref,
                own_ref, coupling_ref, left_ref, slots_x_ref, slots_y_ref):
    p = pl.program_id(0)
    span_x, span_y = slots_x_ref.shape[0], slots_y_ref.shape[0]

    @pl.when(p == 0)
    def _():
        for ref, used, span in ((slots_x_ref, used_x_ref, span_x), (slots_y_ref, used_y_ref, span_y)):
            @pl.loop(0, span)
            def _(k):
                @pl.when(used[k] == 0)
                def _():
                    ref[k] = jnp.zeros(ref.shape[1:], ref.dtype)

    count = counts_ref[p]
    width = coupling_ref.shape[-1]
    rows = lax.broadcasted_iota(jnp.int32, (width, width), 0)
    cols = lax.broadcasted_iota(jnp.int32, (width, width), 1)
    keep = (rows < count) & (cols < count)
    slot = slot_ref[p]
    for t in range(2):
        block = jnp.where(keep, coupling_ref[0, t], jnp.zeros((width, width), coupling_ref.dtype))
        product = jnp.dot(own_ref[...], block, preferred_element_type=jnp.float32).astype(jnp.bfloat16)
        left_ref[0, t] = product
        for ref, mine in ((slots_x_ref, 1), (slots_y_ref, 0)):
            @pl.when((along_ref[p] == mine) & (first_ref[p] == 1))
            def _():
                ref[slot, t] = product

            @pl.when((along_ref[p] == mine) & (first_ref[p] == 0))
            def _():
                ref[slot, t] = (
                    ref[slot, t].astype(jnp.float32) + product.astype(jnp.float32)
                ).astype(jnp.bfloat16)


def left_products(own, coupling, along, slot, first, used_x, used_y, counts):
    pairs, blocks, width, _ = coupling.shape
    modes = own.shape[0]
    span_x, span_y = used_x.shape[0], used_y.shape[0]
    return pl.pallas_call(
        left_kernel,
        grid_spec=pltpu.PrefetchScalarGridSpec(
            num_scalar_prefetch=6,
            grid=(pairs,),
            in_specs=[
                pl.BlockSpec((modes, width), lambda p, *_: (0, 0)),
                pl.BlockSpec((1, blocks, width, width), lambda p, *_: (p, 0, 0, 0)),
            ],
            out_specs=[
                pl.BlockSpec((1, blocks, modes, width), lambda p, *_: (p, 0, 0, 0)),
                pl.BlockSpec((span_x, blocks, modes, width), lambda p, *_: (0, 0, 0, 0),
                             pipeline_mode=pl.Buffered(1)),
                pl.BlockSpec((span_y, blocks, modes, width), lambda p, *_: (0, 0, 0, 0),
                             pipeline_mode=pl.Buffered(1)),
            ],
        ),
        out_shape=[
            jax.ShapeDtypeStruct((pairs, blocks, modes, width), jnp.bfloat16),
            jax.ShapeDtypeStruct((span_x, blocks, modes, width), jnp.bfloat16),
            jax.ShapeDtypeStruct((span_y, blocks, modes, width), jnp.bfloat16),
        ],
        compiler_params=pltpu.CompilerParams(vmem_limit_bytes=40 * 2**20),
        cost_estimate=pl.CostEstimate(flops=2 * pairs * blocks * modes * width * width,
                                      bytes_accessed=30 * 10**6, transcendentals=0),
    )(along, slot, first, used_x, used_y, counts, own, coupling)


def nt(a, b):
    return lax.dot_general(a, b, (((1,), (1,)), ((), ())), preferred_element_type=jnp.float32)


def pair_kernel(along_ref, ix_ref, iy_ref, left_ref, rx_ref, ry_ref, out_ref):
    p = pl.program_id(0)
    for mine, ref in ((1, rx_ref), (0, ry_ref)):
        @pl.when(along_ref[p] == mine)
        def _():
            for t in range(2):
                out_ref[0, t] = nt(left_ref[0, t], ref[0]).astype(jnp.bfloat16)


def pair_products(left, rx, ry, along, ix, iy):
    pairs, blocks, modes, width = left.shape
    return pl.pallas_call(
        pair_kernel,
        grid_spec=pltpu.PrefetchScalarGridSpec(
            num_scalar_prefetch=3,
            grid=(pairs,),
            in_specs=[
                pl.BlockSpec((1, blocks, modes, width), lambda p, *_: (p, 0, 0, 0)),
                pl.BlockSpec((1, modes, width), lambda p, a, ix, iy: (ix[p], 0, 0)),
                pl.BlockSpec((1, modes, width), lambda p, a, ix, iy: (iy[p], 0, 0)),
            ],
            out_specs=pl.BlockSpec((1, blocks, modes, modes), lambda p, *_: (p, 0, 0, 0)),
        ),
        out_shape=jax.ShapeDtypeStruct((pairs, blocks, modes, modes), jnp.bfloat16),
        compiler_params=pltpu.CompilerParams(vmem_limit_bytes=24 * 2**20),
        cost_estimate=pl.CostEstimate(flops=2 * pairs * blocks * modes * width * modes,
                                      bytes_accessed=15 * 10**6, transcendentals=0),
    )(along, ix, iy, left, rx, ry)


def partner_kernel(own_ref, gx_ref, gy_ref, out_ref):
    for t in range(2):
        total = (gx_ref[t].astype(jnp.float32) + gy_ref[t].astype(jnp.float32)).astype(jnp.bfloat16)
        out_ref[t] = nt(own_ref[...], total)


def partner_products(own, gx, gy):
    blocks, modes, width = gx.shape
    return pl.pallas_call(
        partner_kernel,
        out_shape=jax.ShapeDtypeStruct((blocks, modes, modes), jnp.float32),
        compiler_params=pltpu.CompilerParams(vmem_limit_bytes=16 * 2**20),
    )(own, gx, gy)


def body(panels, coupling, partner, counts):
    span_x, span_y = lax.axis_size("sx"), lax.axis_size("sy")
    own = jnp.swapaxes(panels[0], 0, 1)
    along = (partner < span_x).astype(jnp.int32)
    slot = jnp.where(along == 1, partner, partner - span_x)
    order = jnp.arange(partner.shape[0])
    first = jnp.all((partner[:, None] != partner[None, :]) | (order[None, :] >= order[:, None]), axis=1).astype(jnp.int32)
    used = jnp.any(partner[None, :] == jnp.arange(span_x + span_y)[:, None], axis=1).astype(jnp.int32)
    left, slots_x, slots_y = left_products(
        own, coupling, along, slot, first, used[:span_x], used[span_x:], counts
    )
    ry = lax.all_gather(own, "sy", axis=0)
    rx = lax.all_gather(own, "sx", axis=0)
    gy = lax.psum_scatter(slots_y, "sy", scatter_dimension=0, tiled=True)
    gx = lax.psum_scatter(slots_x, "sx", scatter_dimension=0, tiled=True)
    pair_blocks = pair_products(
        left, rx, ry, along, jnp.where(along == 1, slot, 0), jnp.where(along == 1, 0, slot)
    )
    partner_blocks = partner_products(own, gx[0], gy[0])
    return (pair_blocks, partner_blocks[None])


def solution(mesh):
    placed = (
        P(("sx", "sy"), None, None),
        P(("sx", "sy"), None, None, None),
        P(("sx", "sy")),
        P(("sx", "sy")),
    )
    return jax.shard_map(
        body,
        mesh=mesh,
        in_specs=placed,
        out_specs=(P(("sx", "sy"), None, None, None), P(("sx", "sy"), None, None, None)),
        check_vma=False,
    )
```

time: 309 us -> 239 us (0.77)
  matrix products: 72.4 us -> 0 us
  local copies, waits for them, and re-layouts: 38.9 us -> 14.9 us
  Pallas kernels: 0 us -> 23.5 us
  waiting for transfers between devices: 176 us -> 183 us
    dot_general x5 -> x0, matrix products: 72.4 us -> none  [the longest x1 24.3 us: body(): jnp.einsum('pk,ptmn->ktnm', (along_x[:, None] & (partner[:, None] == slot...]
    convert_element_type x2 -> x0, local copies, waits for them, and re-layouts: 38.9 us -> none  [the longest x1 25.6 us: body(): gathered_rows = lax.psum_scatter(jnp.einsum('pk,ptmn->ktnm', (along_x[:,...]
    reduce_scatter x1, waiting for transfers between devices: 0.02 us -> 28 us  [body(): gy = lax.psum_scatter(slots_y, 'sy', scatter_dimension=0, tiled=True)]
    pallas_call x0 -> x3, Pallas kernels: none -> 23.5 us  [the longest x1 14.6 us: left_products(): pl.pallas_call(left_kernel, grid_spec=pltpu.PrefetchScalarGridSpec(num_sc...]
    all_gather x2, waiting for transfers between devices: 79 us -> 62.4 us  [the longest x1 57.2 us: body(): rx = lax.all_gather(own, 'sx', axis=0)]
    unnamed x4 -> x20, local copies, waits for them, and re-layouts: 0.01 us -> 14.8 us
    unnamed x5, waiting for transfers between devices: 97.1 us -> 92.9 us
  transfers between devices with their start and end apart: 4 -> 4, of which waited for: 3 -> 4; matrix products, arithmetic and copies ran while one was open for 19% -> 1% of each run, Pallas kernels for 0% -> 9%
where the time goes in v1:
time: 239 us
  waiting for transfers between devices  183 us (77%)
  Pallas kernels  23.5 us (10%)
  local copies, waits for them, and re-layouts  14.9 us (6%)
  between operations  13.8 us (6%)
  other arithmetic  2.99 us (1%)
    unnamed x5, waiting for transfers between devices  92.9 us
    all_gather x1, waiting for transfers between devices, body(): rx = lax.all_gather(own, 'sx', axis=0)  57.2 us
    reduce_scatter x1, waiting for transfers between devices, body(): gy = lax.psum_scatter(slots_y, 'sy', scatter_dimension=0, tiled=True)  28 us
    unnamed x20, local copies, waits for them, and re-layouts  14.8 us
    pallas_call x1, Pallas kernels, left_products(): pl.pallas_call(left_kernel, grid_spec=pltpu.PrefetchScalarGridSpec(num_sc...  14.6 us
    pallas_call x1, Pallas kernels, pair_products(): pl.pallas_call(pair_kernel, grid_spec=pltpu.PrefetchScalarGridSpec(num_sc...  7.18 us
    all_gather x1, waiting for transfers between devices, body(): ry = lax.all_gather(own, 'sy', axis=0)  5.21 us
  transfers between devices with their start and end apart: 4, of which 4 were waited for; matrix products, arithmetic and copies ran while one was open for 1% of the time, Pallas kernels for 9%

profile of v1, /device:TPU:0, one launch (start us, length us, event | category | flops | bytes accessed | tf_op | source)
XLA Modules:
  0.0 238.7 jit_solution(10589995990789305029)
XLA Ops:
  7.2 0.0 all-gather.7.cloned.1.call-start
  7.2 0.7 all-gather.7.cloned.1.call-update
  7.9 0.0 all-gather.5.cloned.1.call-start
  7.9 0.7 all-gather.5.cloned.1.call-update
  8.6 0.0 reduce-scatter.5.cloned.1.call-start
  8.7 0.7 fusion.2
  9.4 0.1 slice.7.used_y_ref
  9.5 0.9 fusion.1
  10.4 0.7 compare_convert_fusion.along_ref
  11.1 0.7 add_select_fusion
  11.8 0.0 copy-start.3
  11.8 1.0 copy-done.3
  12.7 0.0 copy-start.8
  12.7 2.3 copy-done.8
  15.1 0.0 copy-start.9
  15.1 0.7 copy-done.9
  15.7 14.6 %shard_map.59 = (bf16[8,2,400,384]{3,2,1,0:T(8,128)(2,1)S(1)}, bf16[16,2,400,384]{3,2,1,0:T(8,128)(2,1)}, bf16[8,2,400,384]{3,2,1,0:T(8,128)(2,1)}) custom-call(s32[8]{0:T(128)S(1)} %compare_convert_fusion.along_ref, s32[8]{0:T(128)S(1)} %get-tuple-element.8.slot_ref, s32[8]{0:T(128)S(1)} %convert_element_type.10.first_ref, s32[16]{0:T(128)S(1)} %bitcast.18, ...), custom_call_target="tpu_custom_call" | custom-call | flops 1887436800 | bytes 30000000 | tf_op jit(solution)/shard_map/pallas_call | solution.py:51
  30.3 0.0 copy-start.1
  30.3 2.2 copy-done.1
  32.6 0.0 reduce-scatter.5.cloned.1.call-update
  32.6 0.0 reduce-scatter.7.cloned.1.call-start
  32.6 0.5 reduce-scatter.7.cloned.1.call-update
  33.2 5.2 %all-gather.7.cloned.1.call-done = bf16[3200,384]{1,0:T(8,128)(2,1)} async-done(((bf16[400,384]{1,0:T(8,128)(2,1)}), bf16[3200,384]{1,0:T(8,128)(2,1)}) %all-gather.7.cloned.1.call-update) | async-done | bytes 2457616 | tf_op jit(solution)/shard_map/all_gather | solution.py:139
  38.4 57.2 %all-gather.5.cloned.1.call-done = bf16[6400,384]{1,0:T(8,128)(2,1)} async-done(((bf16[400,384]{1,0:T(8,128)(2,1)}), bf16[6400,384]{1,0:T(8,128)(2,1)}) %all-gather.5.cloned.1.call-update) | async-done | bytes 4915216 | tf_op jit(solution)/shard_map/all_gather | solution.py:140
  95.6 0.0 copy-start
  95.6 2.4 %copy-done = bf16[6400,384]{1,0:T(8,128)(2,1)S(1)} copy-done((bf16[6400,384]{1,0:T(8,128)(2,1)S(1)}, bf16[6400,384]{1,0:T(8,128)(2,1)}, u32[]{:S(2)}) %copy-start) | copy-done | bytes 4915224
  98.0 0.0 copy-start.2
  98.0 2.4 %copy-done.2 = bf16[8,2,400,384]{3,2,1,0:T(8,128)(2,1)S(1)} copy-done((bf16[8,2,400,384]{3,2,1,0:T(8,128)(2,1)S(1)}, bf16[8,2,400,384]{3,2,1,0:T(8,128)(2,1)}, u32[]{:S(2)}) %copy-start.2) | copy-done | bytes 4915224
  100.4 0.0 copy-start.5
  100.4 1.7 copy-done.5
  102.1 0.0 copy-start.4
  102.1 7.2 %shard_map.60 = bf16[8,2,400,400]{3,2,1,0:T(8,128)(2,1)} custom-call(s32[8]{0:T(128)S(1)} %compare_convert_fusion.along_ref, s32[8]{0:T(128)S(1)} %get-tuple-element.10.ix_ref, s32[8]{0:T(128)S(1)} %get-tuple-element.9.iy_ref, bf16[8,2,400,384]{3,2,1,0:T(8,128)(2,1)S(1)} %copy-done.2, bf16[16,400,384]{2,1,0:T(8,128)(2,1)S(1)} %bitcast.10, ...), custom_call_target="tpu_custom_call" | custom-call | flops 1966080000 | bytes 15000000 | tf_op jit(solution)/shard_map/pallas_call | solution.py:94
  109.3 28.0 %reduce-scatter.5.cloned.1.call-done = bf16[1,2,400,384]{3,2,1,0:T(8,128)(2,1)} async-done(((bf16[8,2,400,384]{3,2,1,0:T(8,128)(2,1)}), bf16[1,2,400,384]{3,2,1,0:T(8,128)(2,1)}) %reduce-scatter.5.cloned.1.call-update) | async-done | bytes 614416 | tf_op jit(solution)/shard_map/reduce_scatter | solution.py:141
  137.2 91.0 %reduce-scatter.7.cloned.1.call-done = bf16[1,2,400,384]{3,2,1,0:T(8,128)(2,1)} async-done(((bf16[16,2,400,384]{3,2,1,0:T(8,128)(2,1)}), bf16[1,2,400,384]{3,2,1,0:T(8,128)(2,1)}) %reduce-scatter.7.cloned.1.call-update) | async-done | bytes 614416
  228.3 0.0 copy-done.4
  228.3 0.0 copy-start.6
  228.3 1.1 copy-done.6
  229.3 0.0 copy-start.7
  229.3 1.1 copy-done.7
  230.4 1.8 shard_map.61
  (2 shorter events, 0.0 us)
Async XLA Ops:
  7.2 31.2 %all-gather.7.cloned.1.call-start = ((), (), s32[]{:S(2)}) async-start(), calls=%async_computation.4 | async-start | bytes 2764800 | tf_op jit(solution)/shard_map/all_gather | solution.py:139
  7.9 87.7 %all-gather.5.cloned.1.call-start = ((), (), s32[]{:S(2)}) async-start(), calls=%async_computation.3 | async-start | bytes 5222400 | tf_op jit(solution)/shard_map/all_gather | solution.py:140
  8.6 128.6 %reduce-scatter.5.cloned.1.call-start = ((), (), s32[]{:S(2)}) async-start(), calls=%async_computation.2 | async-start | bytes 5529600 | tf_op jit(solution)/shard_map/reduce_scatter | solution.py:141
  11.8 1.0 copy-start.3
  12.7 2.3 copy-start.8
  15.1 0.7 copy-start.9
  30.3 2.2 copy-start.1
  32.6 195.7 %reduce-scatter.7.cloned.1.call-start = ((), (), s32[]{:S(2)}) async-start(), calls=%async_computation.5 | async-start | bytes 10444800
  95.6 2.4 %copy-start = (bf16[6400,384]{1,0:T(8,128)(2,1)S(1)}, bf16[6400,384]{1,0:T(8,128)(2,1)}, u32[]{:S(2)}) copy-start(bf16[6400,384]{1,0:T(8,128)(2,1)} %all-gather.5.cloned.1.call-done) | copy-start | bytes 14745604
  98.0 2.4 %copy-start.2 = (bf16[8,2,400,384]{3,2,1,0:T(8,128)(2,1)S(1)}, bf16[8,2,400,384]{3,2,1,0:T(8,128)(2,1)}, u32[]{:S(2)}) copy-start(bf16[8,2,400,384]{3,2,1,0:T(8,128)(2,1)} %copy-done.1) | copy-start | bytes 14745604
  100.4 1.7 copy-start.5
  102.1 126.2 %copy-start.4 = (bf16[1,384,400]{1,2,0:T(8,128)(2,1)S(1)}, bf16[1,384,400]{1,2,0:T(8,128)(2,1)}, u32[]{:S(2)}) copy-start(bf16[1,384,400]{1,2,0:T(8,128)(2,1)} %param.4) | copy-start | bytes 921604
  228.3 1.1 copy-start.6
  229.3 1.1 copy-start.7
Sparse Core Ops, SparseCore 0:
  9.7 28.6 all-gather.6
  40.6 54.9 all-gather.4
  98.0 39.1 reduce-scatter.4
  140.6 87.6 reduce-scatter.6

commit v2 on v1

v2 whole, which is shorter than its diff:
```python
import jax
import jax.numpy as jnp
from jax import lax
from jax.experimental import pallas as pl
from jax.experimental.pallas import tpu as pltpu
from jax.sharding import PartitionSpec as P

SIDE = 4
PARTS = ((0, 4), (4, 4), (8, 2), (10, 2), (12, 4))


def slot_of(d1, d2):
    low = d2 < 2
    return jnp.where(
        d1 == 0, 12 + d2,
        jnp.where(d1 == 1, jnp.where(low, 8 + d2, d2),
                  jnp.where(d1 == 2, jnp.where(low, d2, 2 + d2), jnp.where(low, 6 + d2, 8 + d2))))


def offsets(code):
    me = lax.axis_index("sx")
    dx = (code // SIDE - me // SIDE + SIDE) % SIDE
    dy = (code % SIDE - me % SIDE + SIDE) % SIDE
    return dx, dy


def left_kernel(partner_ref, counts_ref, own_ref, coupling_ref, left_ref, *rest):
    outs, (slots_y_ref, slots, used, sems) = rest[:10], rest[10:]
    t, p = pl.program_id(0), pl.program_id(1)
    last = pl.num_programs(1) - 1
    span = SIDE * SIDE
    span_y = slots.shape[0] - span

    @pl.when(p == 0)
    def _():
        @pl.loop(0, span + span_y)
        def _(k):
            used[k] = 0

    modes, width = own_ref.shape
    keep = lax.broadcasted_iota(jnp.int32, (1, width), 1) < counts_ref[p]
    own = jnp.where(keep, own_ref[...], jnp.zeros((modes, width), own_ref.dtype))
    product = jnp.dot(own, coupling_ref[0, 0], preferred_element_type=jnp.float32)
    product = jnp.where(keep, product, 0.0).astype(jnp.bfloat16)
    left_ref[0, 0] = product

    code = partner_ref[p]
    dx, dy = offsets(code)
    slot = jnp.where(code < span, jnp.where(t == 0, slot_of(dx, dy), slot_of(dy, dx)), code)
    fresh = used[slot] == 0

    @pl.when(fresh)
    def _():
        slots[slot, t] = product
        used[slot] = 1

    @pl.when(jnp.logical_not(fresh))
    def _():
        slots[slot, t] = (slots[slot, t].astype(jnp.float32) + product.astype(jnp.float32)).astype(jnp.bfloat16)

    def copies(b):
        return [
            pltpu.make_async_copy(slots.at[pl.ds(at, size), b], outs[5 * b + i], sems.at[5 * b + i])
            for i, (at, size) in enumerate(PARTS)
        ]

    copy_y = pltpu.make_async_copy(slots.at[pl.ds(span, span_y)], slots_y_ref, sems.at[10])

    @pl.when(p == last)
    def _():
        @pl.loop(0, span + span_y)
        def _(k):
            @pl.when(used[k] == 0)
            def _():
                slots[k, t] = jnp.zeros((modes, width), slots.dtype)

        @pl.when(t == 0)
        def _():
            for c in copies(0):
                c.start()

        @pl.when(t == 1)
        def _():
            copy_y.start()
            for c in copies(1):
                c.start()
            for c in copies(0) + copies(1) + [copy_y]:
                c.wait()


def left_products(own, coupling, partner, counts, span_y):
    pairs, blocks, width, _ = coupling.shape
    modes = own.shape[0]
    piece = [jax.ShapeDtypeStruct((size, modes, width), jnp.bfloat16) for _, size in PARTS]
    anywhere = pl.BlockSpec(memory_space=pl.ANY)
    out = pl.pallas_call(
        left_kernel,
        grid_spec=pltpu.PrefetchScalarGridSpec(
            num_scalar_prefetch=2,
            grid=(blocks, pairs),
            in_specs=[
                pl.BlockSpec((modes, width), lambda t, p, *_: (0, 0)),
                pl.BlockSpec((1, 1, width, width), lambda t, p, *_: (p, t, 0, 0)),
            ],
            out_specs=[pl.BlockSpec((1, 1, modes, width), lambda t, p, *_: (p, t, 0, 0))] + [anywhere] * 11,
            scratch_shapes=[
                pltpu.VMEM((SIDE * SIDE + span_y, blocks, modes, width), jnp.bfloat16),
                pltpu.SMEM((SIDE * SIDE + span_y,), jnp.int32),
                pltpu.SemaphoreType.DMA((11,)),
            ],
        ),
        out_shape=[jax.ShapeDtypeStruct((pairs, blocks, modes, width), jnp.bfloat16)] + piece + piece
        + [jax.ShapeDtypeStruct((span_y, blocks, modes, width), jnp.bfloat16)],
        compiler_params=pltpu.CompilerParams(vmem_limit_bytes=24 * 2**20),
        cost_estimate=pl.CostEstimate(flops=2 * pairs * blocks * modes * width * width,
                                      bytes_accessed=25 * 10**6, transcendentals=0),
    )(partner, counts, own, coupling)
    return out[0], out[1:6], out[6:11], out[11]


def nt(a, b):
    return lax.dot_general(a, b, (((1,), (1,)), ((), ())), preferred_element_type=jnp.float32)


def pair_kernel(partner_ref, left_ref, *rest):
    halves, (ry_ref, out_ref, panels, sems) = (rest[:5], rest[5:10]), rest[10:]
    p = pl.program_id(0)
    pairs = panels.shape[0]
    span = SIDE * SIDE
    cut = halves[0][0].shape[1]
    rows = ((0, cut), (cut, panels.shape[1] - cut))

    @pl.when(p == 0)
    def _():
        @pl.loop(0, pairs)
        def _(q):
            code = partner_ref[q]
            dx, dy = offsets(code)

            @pl.when(code >= span)
            def _():
                for h, (at, size) in enumerate(rows):
                    pltpu.make_async_copy(ry_ref.at[code - span, pl.ds(at, size)], panels.at[q, pl.ds(at, size)],
                                          sems.at[q, h]).start()

            for h, (at, size) in enumerate(rows):
                d1, d2 = ((dx, dy), (dy, dx))[h]
                kept, near, far, low, high = halves[h]
                for ref, index, chosen in (
                    (kept, d1, d2 == 0), (near, d1, d2 == 1), (far, d1, d2 == 3),
                    (low, d1, (d2 == 2) & (d1 < 2)), (high, d1 - 2, (d2 == 2) & (d1 >= 2)),
                ):
                    @pl.when((code < span) & chosen)
                    def _():
                        pltpu.make_async_copy(ref.at[index], panels.at[q, pl.ds(at, size)], sems.at[q, h]).start()

    for h, (at, size) in enumerate(rows):
        pltpu.make_async_copy(ry_ref.at[0, pl.ds(at, size)], panels.at[p, pl.ds(at, size)], sems.at[p, h]).wait()
    for t in range(2):
        out_ref[0, t] = nt(left_ref[0, t], panels[p]).astype(jnp.bfloat16)


def pair_products(left, half_a, half_b, ry, partner):
    pairs, blocks, modes, width = left.shape
    anywhere = pl.BlockSpec(memory_space=pl.ANY)
    return pl.pallas_call(
        pair_kernel,
        grid_spec=pltpu.PrefetchScalarGridSpec(
            num_scalar_prefetch=1,
            grid=(pairs,),
            in_specs=[pl.BlockSpec((1, blocks, modes, width), lambda p, *_: (p, 0, 0, 0))] + [anywhere] * 11,
            out_specs=pl.BlockSpec((1, blocks, modes, modes), lambda p, *_: (p, 0, 0, 0)),
            scratch_shapes=[
                pltpu.VMEM((pairs, modes, width), jnp.bfloat16),
                pltpu.SemaphoreType.DMA((pairs, 2)),
            ],
        ),
        out_shape=jax.ShapeDtypeStruct((pairs, blocks, modes, modes), jnp.bfloat16),
        compiler_params=pltpu.CompilerParams(vmem_limit_bytes=16 * 2**20),
        cost_estimate=pl.CostEstimate(flops=2 * pairs * blocks * modes * width * modes,
                                      bytes_accessed=15 * 10**6, transcendentals=0),
    )(partner, left, *half_a, *half_b, ry)


def partner_kernel(own_ref, gy_ref, *rest):
    sums, out_ref = rest[:-1], rest[-1]
    each = len(sums) // 2
    for t in range(2):
        total = gy_ref[t].astype(jnp.float32)
        for ref in sums[t * each:(t + 1) * each]:
            total = total + ref[...].astype(jnp.float32)
        out_ref[t] = nt(own_ref[...], total.astype(jnp.bfloat16))


def partner_products(own, gy, sums):
    blocks, modes, width = gy.shape
    return pl.pallas_call(
        partner_kernel,
        out_shape=jax.ShapeDtypeStruct((blocks, modes, modes), jnp.float32),
        compiler_params=pltpu.CompilerParams(vmem_limit_bytes=16 * 2**20),
    )(own, gy, *sums)


def shift(value, axis, by):
    moved = []
    for x in range(SIDE):
        for y in range(SIDE):
            to = ((x + by) % SIDE * SIDE + y) if axis == 0 else (x * SIDE + (y + by) % SIDE)
            moved.append((x * SIDE + y, to))
    return lax.ppermute(value, "sx", moved)


def gather_half(piece, first):
    second = 1 - first
    kept = jnp.stack([piece] + [shift(piece, first, -d) for d in (1, 2, 3)])
    near = shift(kept, second, -1)
    far = shift(kept, second, 1)
    low = shift(near[:2], second, -1)
    high = shift(far[2:], second, 1)
    return kept, near, far, low, high


def added(*terms):
    return sum(v.astype(jnp.float32) for v in terms).astype(jnp.bfloat16)


def scatter_half(parts, first):
    second = 1 - first
    up, down, pass_up, pass_down, kept = parts
    got_up = shift(up, first, 1)
    got_down = shift(down, first, -1)
    last_up = shift(added(pass_up, got_up[:2]), first, 1)
    last_down = shift(added(pass_down, got_down[:2]), first, -1)
    v = [
        added(kept[0], got_down[2], last_up[0]),
        added(kept[1], got_down[3], last_up[1]),
        added(kept[2], got_up[2], last_down[0]),
        added(kept[3], got_up[3], last_down[1]),
    ]
    return [v[0]] + [shift(v[d], second, d) for d in (1, 2, 3)]


def body(panels, coupling, partner, counts):
    own = jnp.swapaxes(panels[0], 0, 1)
    modes = own.shape[0]
    cut = (modes // 2 + 15) // 16 * 16
    left, parts0, parts1, slots_y = left_products(own, coupling, partner, counts, lax.axis_size("sy"))
    ry = lax.all_gather(own, "sy", axis=0)
    half_a = gather_half(own[:cut], 0)
    half_b = gather_half(own[cut:], 1)
    gy = lax.psum_scatter(slots_y, "sy", scatter_dimension=0, tiled=True)
    sums = scatter_half(parts0, 0) + scatter_half(parts1, 1)
    pair_blocks = pair_products(left, half_a, half_b, ry, partner)
    partner_blocks = partner_products(own, gy[0], sums)
    return (pair_blocks, partner_blocks[None])


def solution(mesh):
    placed = (
        P(("sx", "sy"), None, None),
        P(("sx", "sy"), None, None, None),
        P(("sx", "sy")),
        P(("sx", "sy")),
    )
    return jax.shard_map(
        body,
        mesh=mesh,
        in_specs=placed,
        out_specs=(P(("sx", "sy"), None, None, None), P(("sx", "sy"), None, None, None)),
        check_vma=False,
    )
```

time: 239 us -> 210 us (0.88); the launches traced: 239 us -> 207 us
  waiting for transfers between devices: 183 us -> 88.3 us
  starting transfers between devices: 0.16 us -> 44.2 us
  local copies, waits for them, and re-layouts: 14.9 us -> 30.7 us
  Pallas kernels: 23.5 us -> 26.1 us
    unnamed x5 -> x2, waiting for transfers between devices: 92.9 us -> 0.7 us
    ppermute x0 -> x28, waiting for transfers between devices: none -> 87.6 us  [shift(): return lax.ppermute(value, 'sx', moved)]
    all_gather x1 -> x0, waiting for transfers between devices: 57.2 us -> none  [body(): rx = lax.all_gather(own, 'sx', axis=0)]
    ppermute x0 -> x28, starting transfers between devices: none -> 44.2 us  [shift(): return lax.ppermute(value, 'sx', moved)]
    reduce_scatter x1, waiting for transfers between devices: 28 us -> 0.02 us  [body(): gy = lax.psum_scatter(slots_y, 'sy', scatter_dimension=0, tiled=True)]
    unnamed x20 -> x70, local copies, waits for them, and re-layouts: 14.8 us -> 30.5 us
    all_gather x1, waiting for transfers between devices: 5.21 us -> 0.01 us  [body(): ry = lax.all_gather(own, 'sy', axis=0)]
    pallas_call x1, Pallas kernels: 7.18 us -> 11.2 us  [pair_products(): pl.pallas_call(pair_kernel, grid_spec=pltpu.PrefetchScalarGridSpec(num_sc...]
  transfers between devices with their start and end apart: 4 -> 30, of which waited for: 4 -> 11; matrix products, arithmetic and copies ran while one was open for 1% -> 2% of each run, Pallas kernels for 9% -> 11%
where the time goes in v2:
time: 210 us; the launch traced here: 207 us
  waiting for transfers between devices  88.3 us (42%)
  starting transfers between devices  44.2 us (21%)
  local copies, waits for them, and re-layouts  30.7 us (15%)
  Pallas kernels  26.1 us (12%)
  between operations  14.4 us (7%)
  other arithmetic  3.63 us (2%)
    ppermute x28, waiting for transfers between devices, shift(): return lax.ppermute(value, 'sx', moved)  87.6 us
    ppermute x28, starting transfers between devices, shift(): return lax.ppermute(value, 'sx', moved)  44.2 us
    unnamed x70, local copies, waits for them, and re-layouts  30.5 us
    pallas_call x1, Pallas kernels, left_products(): pl.pallas_call(left_kernel, grid_spec=pltpu.PrefetchScalarGridSpec(num_sc...  11.7 us
    pallas_call x1, Pallas kernels, pair_products(): pl.pallas_call(pair_kernel, grid_spec=pltpu.PrefetchScalarGridSpec(num_sc...  11.2 us
  transfers between devices with their start and end apart: 30, of which 11 were waited for; matrix products, arithmetic and copies ran while one was open for 2% of the time, Pallas kernels for 11%

profile of v2, /device:TPU:0, one launch (start us, length us, event | category | flops | bytes accessed | tf_op | source)
XLA Modules:
  0.0 207.3 jit_solution(7216683278870486834)
XLA Ops:
  8.0 1.0 copy-done.3
  9.6 2.3 %copy-done.33 = bf16[8,2,384,384]{3,2,1,0:T(8,128)(2,1)S(1)} copy-done((bf16[8,2,384,384]{3,2,1,0:T(8,128)(2,1)S(1)}, bf16[8,2,384,384]{3,2,1,0:T(8,128)(2,1)}, u32[]{:S(2)}) %copy-start.33) | copy-done | bytes 4718616
  12.6 11.7 %shard_map.59 = (bf16[8,2,400,384]{3,2,1,0:T(8,128)(2,1)S(1)}, bf16[4,400,384]{2,1,0:T(8,128)(2,1)}, bf16[4,400,384]{2,1,0:T(8,128)(2,1)}, bf16[2,400,384]{2,1,0...) custom-call(s32[8]{0:T(128)S(1)} %copy-done.31, ...), custom_call_target="tpu_custom_call" | custom-call | flops 1887436800 | bytes 25000000 | tf_op jit(solution)/shard_map/pallas_call | solution.py:96
  24.3 2.2 %copy-done = bf16[8,2,400,384]{3,2,1,0:T(8,128)(2,1)} copy-done((bf16[8,2,400,384]{3,2,1,0:T(8,128)(2,1)}, bf16[8,2,400,384]{3,2,1,0:T(8,128)(2,1)S(1)}, u32[]{:S(2)}) %copy-start) | copy-done | bytes 4915224
  26.5 2.2 %copy-done.1 = bf16[8,2,400,384]{3,2,1,0:T(8,128)(2,1)} copy-done((bf16[8,2,400,384]{3,2,1,0:T(8,128)(2,1)}, bf16[8,2,400,384]{3,2,1,0:T(8,128)(2,1)S(1)}, u32[]{:S(2)}) %copy-start.1) | copy-done | bytes 4915224
  28.8 1.1 copy-done.8
  29.9 1.0 copy-done.10
  33.5 1.9 collective-permute-start.22
  35.4 1.5 collective-permute-start.21
  37.5 2.7 %collective-permute-start.7 = (bf16[192,384]{1,0:T(8,128)(2,1)S(1)}, bf16[192,384]{1,0:T(8,128)(2,1)S(1)}, u32[]{:S(2)}, u32[]{:S(2)}) collective-permute-start(bf16[192,384]{1,0:T(8,128)(2,1)S(1)} %get-tuple-element.39), channel_id=1, source_target_pairs={{0,24},{8,0},{16,8},{24,16},{32,56},{40,32},{48,40},{56,48},{64,88... | collective-permute-start | bytes 442376 | tf_op jit(solution)/shard_map/ppermute | solution.py:210
  40.8 26.4 %collective-permute-done.9 = bf16[192,384]{1,0:T(8,128)(2,1)S(1)} collective-permute-done((bf16[192,384]{1,0:T(8,128)(2,1)S(1)}, bf16[192,384]{1,0:T(8,128)(2,1)S(1)}, u32[]{:S(2)}, u32[]{:S(2)}) %collective-permute-start.9) | collective-permute-done | bytes 147488 | tf_op jit(solution)/shard_map/ppermute | solution.py:210
  67.2 1.5 collective-permute-start.15
  68.8 3.8 %collective-permute-start = (bf16[208,384]{1,0:T(8,128)(2,1)S(1)}, bf16[208,384]{1,0:T(8,128)(2,1)S(1)}, u32[]{:S(2)}, u32[]{:S(2)}) collective-permute-start(bf16[208,384]{1,0:T(8,128)(2,1)S(1)} %get-tuple-element.41), channel_id=1, source_target_pairs={{0,96},{8,104},{16,112},{24,120},{32,0},{40,8},{48,16},{56,24},{64... | collective-permute-start | bytes 479240 | tf_op jit(solution)/shard_map/ppermute | solution.py:210
  72.5 2.2 %collective-permute-start.1 = (bf16[208,384]{1,0:T(8,128)(2,1)S(1)}, bf16[208,384]{1,0:T(8,128)(2,1)S(1)}, u32[]{:S(2)}, u32[]{:S(2)}) collective-permute-start(bf16[208,384]{1,0:T(8,128)(2,1)S(1)} %get-tuple-element.41), channel_id=1, source_target_pairs={{0,64},{8,72},{16,80},{24,88},{32,96},{40,104},{48,112},{56,120},{... | collective-permute-start | bytes 479240 | tf_op jit(solution)/shard_map/ppermute | solution.py:210
  74.7 5.4 %collective-permute-done = bf16[208,384]{1,0:T(8,128)(2,1)S(1)} collective-permute-done((bf16[208,384]{1,0:T(8,128)(2,1)S(1)}, bf16[208,384]{1,0:T(8,128)(2,1)S(1)}, u32[]{:S(2)}, u32[]{:S(2)}) %collective-permute-start) | collective-permute-done | bytes 159776 | tf_op jit(solution)/shard_map/ppermute | solution.py:210
  80.1 3.8 %collective-permute-start.14 = (bf16[4,400,384]{2,1,0:T(8,128)(2,1)}, bf16[4,400,384]{2,1,0:T(8,128)(2,1)S(1)}, u32[]{:S(2)}, u32[]{:S(2)}) collective-permute-start(bf16[4,400,384]{2,1,0:T(8,128)(2,1)} %get-tuple-element.17), channel_id=1, source_target_pairs={{0,96},{8,104},{16,112},{24,120},{32,0},{40,8},{48,16},{56,24},{64... | collective-permute-start | bytes 3686408 | tf_op jit(solution)/shard_map/ppermute | solution.py:210
  83.9 17.5 %collective-permute-done.1 = bf16[208,384]{1,0:T(8,128)(2,1)S(1)} collective-permute-done((bf16[208,384]{1,0:T(8,128)(2,1)S(1)}, bf16[208,384]{1,0:T(8,128)(2,1)S(1)}, u32[]{:S(2)}, u32[]{:S(2)}) %collective-permute-start.1) | collective-permute-done | bytes 159776 | tf_op jit(solution)/shard_map/ppermute | solution.py:210
  101.5 6.4 %collective-permute-done.2 = bf16[208,384]{1,0:T(8,128)(2,1)S(1)} collective-permute-done((bf16[208,384]{1,0:T(8,128)(2,1)S(1)}, bf16[208,384]{1,0:T(8,128)(2,1)S(1)}, u32[]{:S(2)}, u32[]{:S(2)}) %collective-permute-start.2) | collective-permute-done | bytes 159776 | tf_op jit(solution)/shard_map/ppermute | solution.py:210
  108.0 3.3 %collective-permute-start.3 = (bf16[4,208,384]{2,1,0:T(8,128)(2,1)S(1)}, bf16[4,208,384]{2,1,0:T(8,128)(2,1)S(1)}, u32[]{:S(2)}, u32[]{:S(2)}) collective-permute-start(bf16[4,208,384]{2,1,0:T(8,128)(2,1)S(1)} %pad_maximum_fusion.rest_0_), channel_id=1, source_target_pairs={{0,24},{8,0},{16,8},{24,16},{32,56},{40,32},{48,40},{56,48},{64,88... | collective-permute-start | bytes 1916936 | tf_op jit(solution)/shard_map/ppermute | solution.py:210
  111.8 7.5 %collective-permute-done.10.rest_6_ = bf16[4,192,384]{2,1,0:T(8,128)(2,1)S(1)} collective-permute-done((bf16[4,192,384]{2,1,0:T(8,128)(2,1)S(1)}, bf16[4,192,384]{2,1,0:T(8,128)(2,1)S(1)}, u32[]{:S(2)}, u32[]{:S(2)}) %collective-permute-start.10) | collective-permute-done | bytes 589856 | tf_op jit(solution)/shard_map/ppermute | solution.py:210
  119.3 3.2 %collective-permute-start.25 = (bf16[2,400,384]{2,1,0:T(8,128)(2,1)S(1)}, bf16[2,400,384]{2,1,0:T(8,128)(2,1)S(1)}, u32[]{:S(2)}, u32[]{:S(2)}) collective-permute-start(bf16[2,400,384]{2,1,0:T(8,128)(2,1)S(1)} %add_convert_fusion), channel_id=1, source_target_pairs={{0,24},{8,0},{16,8},{24,16},{32,56},{40,32},{48,40},{56,48},{64,88... | collective-permute-start | bytes 1843208 | tf_op jit(solution)/shard_map/ppermute | solution.py:210
  123.9 2.4 %collective-permute-start.18 = (bf16[2,400,384]{2,1,0:T(8,128)(2,1)S(1)}, bf16[2,400,384]{2,1,0:T(8,128)(2,1)S(1)}, u32[]{:S(2)}, u32[]{:S(2)}) collective-permute-start(bf16[2,400,384]{2,1,0:T(8,128)(2,1)S(1)} %add_convert_fusion.2), channel_id=1, source_target_pairs={{0,96},{8,104},{16,112},{24,120},{32,0},{40,8},{48,16},{56,24},{64... | collective-permute-start | bytes 1843208 | tf_op jit(solution)/shard_map/ppermute | solution.py:210
  126.3 2.3 %collective-permute-done.4.rest_2_ = bf16[4,208,384]{2,1,0:T(8,128)(2,1)S(1)} collective-permute-done((bf16[4,208,384]{2,1,0:T(8,128)(2,1)S(1)}, bf16[4,208,384]{2,1,0:T(8,128)(2,1)S(1)}, u32[]{:S(2)}, u32[]{:S(2)}) %collective-permute-start.4) | collective-permute-done | bytes 639008 | tf_op jit(solution)/shard_map/ppermute | solution.py:210
  128.6 3.2 %collective-permute-start.11 = (bf16[4,192,384]{2,1,0:T(8,128)(2,1)S(1)}, bf16[4,192,384]{2,1,0:T(8,128)(2,1)S(1)}, u32[]{:S(2)}, u32[]{:S(2)}) collective-permute-start(bf16[4,192,384]{2,1,0:T(8,128)(2,1)S(1)} %pad_maximum_fusion.1.rest_5_), channel_id=1, source_target_pairs={{0,32},{8,40},{16,48},{24,56},{32,64},{40,72},{48,80},{56,88},{64,... | collective-permute-start | bytes 1769480 | tf_op jit(solution)/shard_map/ppermute | solution.py:210
  131.9 5.9 %collective-permute-done.23 = bf16[2,400,384]{2,1,0:T(8,128)(2,1)S(1)} collective-permute-done((bf16[2,400,384]{2,1,0:T(8,128)(2,1)S(1)}, bf16[2,400,384]{2,1,0:T(8,128)(2,1)S(1)}, u32[]{:S(2)}, u32[]{:S(2)}) %collective-permute-start.23) | collective-permute-done | bytes 614432 | tf_op jit(solution)/shard_map/ppermute | solution.py:210
  137.8 2.0 collective-permute-start.6
  139.8 1.3 fusion.7
  141.2 8.3 %collective-permute-done.11.rest_7_ = bf16[4,192,384]{2,1,0:T(8,128)(2,1)S(1)} collective-permute-done((bf16[4,192,384]{2,1,0:T(8,128)(2,1)S(1)}, bf16[4,192,384]{2,1,0:T(8,128)(2,1)S(1)}, u32[]{:S(2)}, u32[]{:S(2)}) %collective-permute-start.11) | collective-permute-done | bytes 589856 | tf_op jit(solution)/shard_map/ppermute | solution.py:210
  149.5 3.3 %collective-permute-start.12 = (bf16[2,192,384]{2,1,0:T(8,128)(2,1)S(1)}, bf16[2,192,384]{2,1,0:T(8,128)(2,1)S(1)}, u32[]{:S(2)}, u32[]{:S(2)}) collective-permute-start(bf16[2,192,384]{2,1,0:T(8,128)(2,1)S(1)} %slice.140), channel_id=1, source_target_pairs={{0,96},{8,104},{16,112},{24,120},{32,0},{40,8},{48,16},{56,24},{64... | collective-permute-start | bytes 884744 | tf_op jit(solution)/shard_map/ppermute | solution.py:210
  153.0 1.4 fusion.3
  154.4 6.8 %collective-permute-done.12.rest_8_ = bf16[2,192,384]{2,1,0:T(8,128)(2,1)S(1)} collective-permute-done((bf16[2,192,384]{2,1,0:T(8,128)(2,1)S(1)}, bf16[2,192,384]{2,1,0:T(8,128)(2,1)S(1)}, u32[]{:S(2)}, u32[]{:S(2)}) %collective-permute-start.12) | collective-permute-done | bytes 294944 | tf_op jit(solution)/shard_map/ppermute | solution.py:210
  161.9 1.9 collective-permute-start.26
  164.7 2.5 %collective-permute-start.27 = (bf16[400,384]{1,0:T(8,128)(2,1)}, bf16[400,384]{1,0:T(8,128)(2,1)}, u32[]{:S(2)}, u32[]{:S(2)}) collective-permute-start(bf16[400,384]{1,0:T(8,128)(2,1)} %get-tuple-element.26), channel_id=1, source_target_pairs={{0,96},{8,104},{16,112},{24,120},{32,0},{40,8},{48,16},{56,24},{64... | collective-permute-start | bytes 921608 | tf_op jit(solution)/shard_map/ppermute | solution.py:210
  168.7 2.0 collective-permute-start.19
  171.4 1.6 collective-permute-start.20
  173.0 2.4 %copy-done.2 = bf16[8,2,400,384]{3,2,1,0:T(8,128)(2,1)S(1)} copy-done((bf16[8,2,400,384]{3,2,1,0:T(8,128)(2,1)S(1)}, bf16[8,2,400,384]{3,2,1,0:T(8,128)(2,1)}, u32[]{:S(2)}) %copy-start.2) | copy-done | bytes 4915224
  175.4 1.7 copy-done.5
  177.1 1.1 copy-done.7
  178.1 1.0 copy-done.22
  179.1 1.0 copy-done.24
  180.1 1.0 copy-done.28
  181.0 1.0 copy-done.30
  182.0 11.2 %shard_map.60 = bf16[8,2,400,400]{3,2,1,0:T(8,128)(2,1)} custom-call(s32[8]{0:T(128)S(1)} %copy-done.32, bf16[8,2,400,384]{3,2,1,0:T(8,128)(2,1)S(1)} %copy-done.2, bf16[4,208,384]{2,1,0:T(8,128)(2,1)S(1)} %pad_maximum_fusion.rest_0_, bf16[4,208,384]{2,1,0:T(8,128)(2,1)S(1)} %collective-permute-done.3.rest_1_, ...), custom_call_target="tpu_custom_call" | custom-call | flops 1966080000 | bytes 15000000 | tf_op jit(solution)/shard_map/pallas_call | solution.py:166
  193.3 1.0 copy-done.12
  194.2 1.0 copy-done.13
  195.2 1.1 copy-done.20
  196.3 1.0 copy-done.26
  197.2 3.2 %shard_map.61 = f32[2,400,400]{2,1,0:T(8,128)} custom-call(bf16[400,384]{1,0:T(8,128)(2,1)S(1)} %bitcast.36, bf16[2,400,384]{2,1,0:T(8,128)(2,1)S(1)} %bitcast.38, bf16[400,384]{1,0:T(8,128)(2,1)S(1)} %copy-done.13, bf16[400,384]{1,0:T(8,128)(2,1)} %collective-permute-done.17.rest_1_, bf16[400,384]{1,0:T(8,128)(2,1)} %collective-permute-done.19.rest_2_, ...), custom_call_target="tpu_custom_call" | custom-call | tf_op jit(solution)/shard_map/pallas_call | solution.py:197
  (101 shorter events, 11.9 us)
Async XLA Ops:
  7.2 165.8 %all-gather.3.cloned.1.call-start = ((), (), s32[]{:S(2)}) async-start(), calls=%async_computation.2 | async-start | bytes 2764800 | tf_op jit(solution)/shard_map/all_gather | solution.py:248
  7.9 185.4 %reduce-scatter.2.cloned.1.call-start = ((), (), s32[]{:S(2)}) async-start(), calls=%async_computation.1 | async-start | bytes 5529600 | tf_op jit(solution)/shard_map/reduce_scatter | solution.py:251
  9.6 2.3 %copy-start.33 = (bf16[8,2,384,384]{3,2,1,0:T(8,128)(2,1)S(1)}, bf16[8,2,384,384]{3,2,1,0:T(8,128)(2,1)}, u32[]{:S(2)}) copy-start(bf16[8,2,384,384]{3,2,1,0:T(8,128)(2,1)} %coupling_ref.1) | copy-start | bytes 14155780
  24.3 2.3 %copy-start = (bf16[8,2,400,384]{3,2,1,0:T(8,128)(2,1)}, bf16[8,2,400,384]{3,2,1,0:T(8,128)(2,1)S(1)}, u32[]{:S(2)}) copy-start(bf16[8,2,400,384]{3,2,1,0:T(8,128)(2,1)S(1)} %get-tuple-element.15) | copy-start | bytes 14745604
  26.5 2.2 %copy-start.1 = (bf16[8,2,400,384]{3,2,1,0:T(8,128)(2,1)}, bf16[8,2,400,384]{3,2,1,0:T(8,128)(2,1)S(1)}, u32[]{:S(2)}) copy-start(bf16[8,2,400,384]{3,2,1,0:T(8,128)(2,1)S(1)} %get-tuple-element.14.left_ref) | copy-start | bytes 14745604
  28.8 1.1 copy-start.8
  29.9 1.0 copy-start.10
  33.5 3.4 %copy-start.4 = (bf16[1,384,400]{1,2,0:T(8,128)(2,1)S(1)}, bf16[1,384,400]{1,2,0:T(8,128)(2,1)}, u32[]{:S(2)}) copy-start(bf16[1,384,400]{1,2,0:T(8,128)(2,1)} %param.4) | copy-start | bytes 921604
  33.5 74.5 %collective-permute-start.22 = (bf16[4,400,384]{2,1,0:T(8,128)(2,1)}, bf16[4,400,384]{2,1,0:T(8,128)(2,1)S(1)}, u32[]{:S(2)}, u32[]{:S(2)}) collective-permute-start(bf16[4,400,384]{2,1,0:T(8,128)(2,1)} %get-tuple-element.24), channel_id=1, source_target_pairs={{0,8},{8,16},{16,24},{24,0},{32,40},{40,48},{48,56},{56,32},{64,72... | collective-permute-start | bytes 3686408 | tf_op jit(solution)/shard_map/ppermute | solution.py:210
  35.4 76.1 %collective-permute-start.21 = (bf16[4,400,384]{2,1,0:T(8,128)(2,1)}, bf16[4,400,384]{2,1,0:T(8,128)(2,1)S(1)}, u32[]{:S(2)}, u32[]{:S(2)}) collective-permute-start(bf16[4,400,384]{2,1,0:T(8,128)(2,1)} %get-tuple-element.22), channel_id=1, source_target_pairs={{0,24},{8,0},{16,8},{24,16},{32,56},{40,32},{48,40},{56,48},{64,88... | collective-permute-start | bytes 3686408 | tf_op jit(solution)/shard_map/ppermute | solution.py:210
  36.9 30.3 %collective-permute-start.9 = (bf16[192,384]{1,0:T(8,128)(2,1)S(1)}, bf16[192,384]{1,0:T(8,128)(2,1)S(1)}, u32[]{:S(2)}, u32[]{:S(2)}) collective-permute-start(bf16[192,384]{1,0:T(8,128)(2,1)S(1)} %get-tuple-element.39), channel_id=1, source_target_pairs={{0,8},{8,16},{16,24},{24,0},{32,40},{40,48},{48,56},{56,32},{64,72... | collective-permute-start | bytes 442376 | tf_op jit(solution)/shard_map/ppermute | solution.py:210
  37.5 31.2 %collective-permute-start.7 = (bf16[192,384]{1,0:T(8,128)(2,1)S(1)}, bf16[192,384]{1,0:T(8,128)(2,1)S(1)}, u32[]{:S(2)}, u32[]{:S(2)}) collective-permute-start(bf16[192,384]{1,0:T(8,128)(2,1)S(1)} %get-tuple-element.39), channel_id=1, source_target_pairs={{0,24},{8,0},{16,8},{24,16},{32,56},{40,32},{48,40},{56,48},{64,88... | collective-permute-start | bytes 442376 | tf_op jit(solution)/shard_map/ppermute | solution.py:210
  40.3 32.3 %collective-permute-start.8 = (bf16[192,384]{1,0:T(8,128)(2,1)S(1)}, bf16[192,384]{1,0:T(8,128)(2,1)S(1)}, u32[]{:S(2)}, u32[]{:S(2)}) collective-permute-start(bf16[192,384]{1,0:T(8,128)(2,1)S(1)} %get-tuple-element.39), channel_id=1, source_target_pairs={{0,16},{8,24},{16,0},{24,8},{32,48},{40,56},{48,32},{56,40},{64,80... | collective-permute-start | bytes 442376 | tf_op jit(solution)/shard_map/ppermute | solution.py:210
  67.2 52.1 %collective-permute-start.15 = (bf16[4,400,384]{2,1,0:T(8,128)(2,1)}, bf16[4,400,384]{2,1,0:T(8,128)(2,1)S(1)}, u32[]{:S(2)}, u32[]{:S(2)}) collective-permute-start(bf16[4,400,384]{2,1,0:T(8,128)(2,1)} %get-tuple-element.19), channel_id=1, source_target_pairs={{0,32},{8,40},{16,48},{24,56},{32,64},{40,72},{48,80},{56,88},{64,... | collective-permute-start | bytes 3686408 | tf_op jit(solution)/shard_map/ppermute | solution.py:210
  68.8 11.3 %collective-permute-start = (bf16[208,384]{1,0:T(8,128)(2,1)S(1)}, bf16[208,384]{1,0:T(8,128)(2,1)S(1)}, u32[]{:S(2)}, u32[]{:S(2)}) collective-permute-start(bf16[208,384]{1,0:T(8,128)(2,1)S(1)} %get-tuple-element.41), channel_id=1, source_target_pairs={{0,96},{8,104},{16,112},{24,120},{32,0},{40,8},{48,16},{56,24},{64... | collective-permute-start | bytes 479240 | tf_op jit(solution)/shard_map/ppermute | solution.py:210
  72.5 28.9 %collective-permute-start.1 = (bf16[208,384]{1,0:T(8,128)(2,1)S(1)}, bf16[208,384]{1,0:T(8,128)(2,1)S(1)}, u32[]{:S(2)}, u32[]{:S(2)}) collective-permute-start(bf16[208,384]{1,0:T(8,128)(2,1)S(1)} %get-tuple-element.41), channel_id=1, source_target_pairs={{0,64},{8,72},{16,80},{24,88},{32,96},{40,104},{48,112},{56,120},{... | collective-permute-start | bytes 479240 | tf_op jit(solution)/shard_map/ppermute | solution.py:210
  80.1 42.6 %collective-permute-start.14 = (bf16[4,400,384]{2,1,0:T(8,128)(2,1)}, bf16[4,400,384]{2,1,0:T(8,128)(2,1)S(1)}, u32[]{:S(2)}, u32[]{:S(2)}) collective-permute-start(bf16[4,400,384]{2,1,0:T(8,128)(2,1)} %get-tuple-element.17), channel_id=1, source_target_pairs={{0,96},{8,104},{16,112},{24,120},{32,0},{40,8},{48,16},{56,24},{64... | collective-permute-start | bytes 3686408 | tf_op jit(solution)/shard_map/ppermute | solution.py:210
  101.4 6.5 %collective-permute-start.2 = (bf16[208,384]{1,0:T(8,128)(2,1)S(1)}, bf16[208,384]{1,0:T(8,128)(2,1)S(1)}, u32[]{:S(2)}, u32[]{:S(2)}) collective-permute-start(bf16[208,384]{1,0:T(8,128)(2,1)S(1)} %get-tuple-element.41), channel_id=1, source_target_pairs={{0,32},{8,40},{16,48},{24,56},{32,64},{40,72},{48,80},{56,88},{64,... | collective-permute-start | bytes 479240 | tf_op jit(solution)/shard_map/ppermute | solution.py:210
  107.9 11.4 %collective-permute-start.10 = (bf16[4,192,384]{2,1,0:T(8,128)(2,1)S(1)}, bf16[4,192,384]{2,1,0:T(8,128)(2,1)S(1)}, u32[]{:S(2)}, u32[]{:S(2)}) collective-permute-start(bf16[4,192,384]{2,1,0:T(8,128)(2,1)S(1)} %pad_maximum_fusion.1.rest_5_), channel_id=1, source_target_pairs={{0,96},{8,104},{16,112},{24,120},{32,0},{40,8},{48,16},{56,24},{64... | collective-permute-start | bytes 1769480 | tf_op jit(solution)/shard_map/ppermute | solution.py:210
  108.0 3.6 %copy-start.19 = (bf16[2,400,384]{2,1,0:T(8,128)(2,1)S(1)}, bf16[2,400,384]{2,1,0:T(8,128)(2,1)}, u32[]{:S(2)}) copy-start(bf16[2,400,384]{2,1,0:T(8,128)(2,1)} %copy-done.18) | copy-start | bytes 1843204
  108.0 15.9 %collective-permute-start.3 = (bf16[4,208,384]{2,1,0:T(8,128)(2,1)S(1)}, bf16[4,208,384]{2,1,0:T(8,128)(2,1)S(1)}, u32[]{:S(2)}, u32[]{:S(2)}) collective-permute-start(bf16[4,208,384]{2,1,0:T(8,128)(2,1)S(1)} %pad_maximum_fusion.rest_0_), channel_id=1, source_target_pairs={{0,24},{8,0},{16,8},{24,16},{32,56},{40,32},{48,40},{56,48},{64,88... | collective-permute-start | bytes 1916936 | tf_op jit(solution)/shard_map/ppermute | solution.py:210
  111.5 11.1 %copy-start.17 = (bf16[2,400,384]{2,1,0:T(8,128)(2,1)S(1)}, bf16[2,400,384]{2,1,0:T(8,128)(2,1)}, u32[]{:S(2)}) copy-start(bf16[2,400,384]{2,1,0:T(8,128)(2,1)} %copy-done.16) | copy-start | bytes 1843204
  111.5 17.1 %collective-permute-start.4 = (bf16[4,208,384]{2,1,0:T(8,128)(2,1)S(1)}, bf16[4,208,384]{2,1,0:T(8,128)(2,1)S(1)}, u32[]{:S(2)}, u32[]{:S(2)}) collective-permute-start(bf16[4,208,384]{2,1,0:T(8,128)(2,1)S(1)} %pad_maximum_fusion.rest_0_), channel_id=1, source_target_pairs={{0,8},{8,16},{16,24},{24,0},{32,40},{40,48},{48,56},{56,32},{64,72... | collective-permute-start | bytes 1916936 | tf_op jit(solution)/shard_map/ppermute | solution.py:210
  111.8 11.1 %copy-start.15 = (bf16[2,400,384]{2,1,0:T(8,128)(2,1)S(1)}, bf16[2,400,384]{2,1,0:T(8,128)(2,1)}, u32[]{:S(2)}) copy-start(bf16[2,400,384]{2,1,0:T(8,128)(2,1)} %copy-done.14) | copy-start | bytes 1843204
  119.3 18.5 %collective-permute-start.23 = (bf16[2,400,384]{2,1,0:T(8,128)(2,1)S(1)}, bf16[2,400,384]{2,1,0:T(8,128)(2,1)S(1)}, u32[]{:S(2)}, u32[]{:S(2)}) collective-permute-start(bf16[2,400,384]{2,1,0:T(8,128)(2,1)S(1)} %add_convert_fusion.1), channel_id=1, source_target_pairs={{0,8},{8,16},{16,24},{24,0},{32,40},{40,48},{48,56},{56,32},{64,72... | collective-permute-start | bytes 1843208 | tf_op jit(solution)/shard_map/ppermute | solution.py:210
  119.3 18.5 %collective-permute-start.25 = (bf16[2,400,384]{2,1,0:T(8,128)(2,1)S(1)}, bf16[2,400,384]{2,1,0:T(8,128)(2,1)S(1)}, u32[]{:S(2)}, u32[]{:S(2)}) collective-permute-start(bf16[2,400,384]{2,1,0:T(8,128)(2,1)S(1)} %add_convert_fusion), channel_id=1, source_target_pairs={{0,24},{8,0},{16,8},{24,16},{32,56},{40,32},{48,40},{56,48},{64,88... | collective-permute-start | bytes 1843208 | tf_op jit(solution)/shard_map/ppermute | solution.py:210
  122.7 26.8 %collective-permute-start.16 = (bf16[2,400,384]{2,1,0:T(8,128)(2,1)S(1)}, bf16[2,400,384]{2,1,0:T(8,128)(2,1)S(1)}, u32[]{:S(2)}, u32[]{:S(2)}) collective-permute-start(bf16[2,400,384]{2,1,0:T(8,128)(2,1)S(1)} %add_convert_fusion.3), channel_id=1, source_target_pairs={{0,32},{8,40},{16,48},{24,56},{32,64},{40,72},{48,80},{56,88},{64,... | collective-permute-start | bytes 1843208 | tf_op jit(solution)/shard_map/ppermute | solution.py:210
  122.8 17.0 %copy-start.11 = (bf16[4,400,384]{2,1,0:T(8,128)(2,1)S(1)}, bf16[4,400,384]{2,1,0:T(8,128)(2,1)}, u32[]{:S(2)}) copy-start(bf16[4,400,384]{2,1,0:T(8,128)(2,1)} %copy-done.10) | copy-start | bytes 3686404
  123.9 28.9 %collective-permute-start.18 = (bf16[2,400,384]{2,1,0:T(8,128)(2,1)S(1)}, bf16[2,400,384]{2,1,0:T(8,128)(2,1)S(1)}, u32[]{:S(2)}, u32[]{:S(2)}) collective-permute-start(bf16[2,400,384]{2,1,0:T(8,128)(2,1)S(1)} %add_convert_fusion.2), channel_id=1, source_target_pairs={{0,96},{8,104},{16,112},{24,120},{32,0},{40,8},{48,16},{56,24},{64... | collective-permute-start | bytes 1843208 | tf_op jit(solution)/shard_map/ppermute | solution.py:210
  128.6 20.8 %collective-permute-start.11 = (bf16[4,192,384]{2,1,0:T(8,128)(2,1)S(1)}, bf16[4,192,384]{2,1,0:T(8,128)(2,1)S(1)}, u32[]{:S(2)}, u32[]{:S(2)}) collective-permute-start(bf16[4,192,384]{2,1,0:T(8,128)(2,1)S(1)} %pad_maximum_fusion.1.rest_5_), channel_id=1, source_target_pairs={{0,32},{8,40},{16,48},{24,56},{32,64},{40,72},{48,80},{56,88},{64,... | collective-permute-start | bytes 1769480 | tf_op jit(solution)/shard_map/ppermute | solution.py:210
  137.8 29.4 %collective-permute-start.5 = (bf16[2,208,384]{2,1,0:T(8,128)(2,1)S(1)}, bf16[2,208,384]{2,1,0:T(8,128)(2,1)S(1)}, u32[]{:S(2)}, u32[]{:S(2)}) collective-permute-start(bf16[2,208,384]{2,1,0:T(8,128)(2,1)S(1)} %slice.137), channel_id=1, source_target_pairs={{0,24},{8,0},{16,8},{24,16},{32,56},{40,32},{48,40},{56,48},{64,88... | collective-permute-start | bytes 958472 | tf_op jit(solution)/shard_map/ppermute | solution.py:210
  137.8 30.1 %collective-permute-start.6 = (bf16[2,208,384]{2,1,0:T(8,128)(2,1)S(1)}, bf16[2,208,384]{2,1,0:T(8,128)(2,1)S(1)}, u32[]{:S(2)}, u32[]{:S(2)}) collective-permute-start(bf16[2,208,384]{2,1,0:T(8,128)(2,1)S(1)} %slice.138), channel_id=1, source_target_pairs={{0,8},{8,16},{16,24},{24,0},{32,40},{40,48},{48,56},{56,32},{64,72... | collective-permute-start | bytes 958472 | tf_op jit(solution)/shard_map/ppermute | solution.py:210
  139.8 13.1 %copy-start.9 = (bf16[4,400,384]{2,1,0:T(8,128)(2,1)S(1)}, bf16[4,400,384]{2,1,0:T(8,128)(2,1)}, u32[]{:S(2)}) copy-start(bf16[4,400,384]{2,1,0:T(8,128)(2,1)} %copy-done.8) | copy-start | bytes 3686404
  149.5 5.0 %copy-start.6 = (bf16[4,192,384]{2,1,0:T(8,128)(2,1)}, bf16[4,192,384]{2,1,0:T(8,128)(2,1)S(1)}, u32[]{:S(2)}) copy-start(bf16[4,192,384]{2,1,0:T(8,128)(2,1)S(1)} %collective-permute-done.11.rest_7_) | copy-start | bytes 1769476
  149.5 21.2 %collective-permute-start.24 = (bf16[400,384]{1,0:T(8,128)(2,1)S(1)}, bf16[400,384]{1,0:T(8,128)(2,1)S(1)}, u32[]{:S(2)}, u32[]{:S(2)}) collective-permute-start(bf16[400,384]{1,0:T(8,128)(2,1)S(1)} %get-tuple-element.35), channel_id=1, source_target_pairs={{0,32},{8,40},{16,48},{24,56},{32,64},{40,72},{48,80},{56,88},{64,... | collective-permute-start | bytes 921608 | tf_op jit(solution)/shard_map/ppermute | solution.py:210
  149.5 11.7 %collective-permute-start.12 = (bf16[2,192,384]{2,1,0:T(8,128)(2,1)S(1)}, bf16[2,192,384]{2,1,0:T(8,128)(2,1)S(1)}, u32[]{:S(2)}, u32[]{:S(2)}) collective-permute-start(bf16[2,192,384]{2,1,0:T(8,128)(2,1)S(1)} %slice.140), channel_id=1, source_target_pairs={{0,96},{8,104},{16,112},{24,120},{32,0},{40,8},{48,16},{56,24},{64... | collective-permute-start | bytes 884744 | tf_op jit(solution)/shard_map/ppermute | solution.py:210
  152.8 11.1 %collective-permute-start.13 = (bf16[2,192,384]{2,1,0:T(8,128)(2,1)S(1)}, bf16[2,192,384]{2,1,0:T(8,128)(2,1)S(1)}, u32[]{:S(2)}, u32[]{:S(2)}) collective-permute-start(bf16[2,192,384]{2,1,0:T(8,128)(2,1)S(1)} %slice.141), channel_id=1, source_target_pairs={{0,32},{8,40},{16,48},{24,56},{32,64},{40,72},{48,80},{56,88},{64,... | collective-permute-start | bytes 884744 | tf_op jit(solution)/shard_map/ppermute | solution.py:210
  152.9 20.0 %copy-start.32 = (s32[8]{0:T(128)S(1)}, s32[8]{0:T(128)}, u32[]{:S(2)}) copy-start(s32[8]{0:T(128)} %partner_ref.3) | copy-start | bytes 100
  161.9 31.3 %collective-permute-start.26 = (bf16[400,384]{1,0:T(8,128)(2,1)}, bf16[400,384]{1,0:T(8,128)(2,1)}, u32[]{:S(2)}, u32[]{:S(2)}) collective-permute-start(bf16[400,384]{1,0:T(8,128)(2,1)} %get-tuple-element.27), channel_id=1, source_target_pairs={{0,64},{8,72},{16,80},{24,88},{32,96},{40,104},{48,112},{56,120},{... | collective-permute-start | bytes 921608 | tf_op jit(solution)/shard_map/ppermute | solution.py:210
  164.7 28.5 %collective-permute-start.27 = (bf16[400,384]{1,0:T(8,128)(2,1)}, bf16[400,384]{1,0:T(8,128)(2,1)}, u32[]{:S(2)}, u32[]{:S(2)}) collective-permute-start(bf16[400,384]{1,0:T(8,128)(2,1)} %get-tuple-element.26), channel_id=1, source_target_pairs={{0,96},{8,104},{16,112},{24,120},{32,0},{40,8},{48,16},{56,24},{64... | collective-permute-start | bytes 921608 | tf_op jit(solution)/shard_map/ppermute | solution.py:210
  167.9 25.3 %collective-permute-start.17 = (bf16[400,384]{1,0:T(8,128)(2,1)}, bf16[400,384]{1,0:T(8,128)(2,1)}, u32[]{:S(2)}, u32[]{:S(2)}) collective-permute-start(bf16[400,384]{1,0:T(8,128)(2,1)} %get-tuple-element.37), channel_id=1, source_target_pairs={{0,8},{8,16},{16,24},{24,0},{32,40},{40,48},{48,56},{56,32},{64,72... | collective-permute-start | bytes 921608 | tf_op jit(solution)/shard_map/ppermute | solution.py:210
  168.7 24.5 %collective-permute-start.19 = (bf16[400,384]{1,0:T(8,128)(2,1)}, bf16[400,384]{1,0:T(8,128)(2,1)}, u32[]{:S(2)}, u32[]{:S(2)}) collective-permute-start(bf16[400,384]{1,0:T(8,128)(2,1)} %get-tuple-element.31), channel_id=1, source_target_pairs={{0,16},{8,24},{16,0},{24,8},{32,48},{40,56},{48,32},{56,40},{64,80... | collective-permute-start | bytes 921608 | tf_op jit(solution)/shard_map/ppermute | solution.py:210
  171.4 21.8 %collective-permute-start.20 = (bf16[400,384]{1,0:T(8,128)(2,1)}, bf16[400,384]{1,0:T(8,128)(2,1)}, u32[]{:S(2)}, u32[]{:S(2)}) collective-permute-start(bf16[400,384]{1,0:T(8,128)(2,1)} %get-tuple-element.30), channel_id=1, source_target_pairs={{0,24},{8,0},{16,8},{24,16},{32,56},{40,32},{48,40},{56,48},{64,88... | collective-permute-start | bytes 921608 | tf_op jit(solution)/shard_map/ppermute | solution.py:210
  173.0 2.4 %copy-start.2 = (bf16[8,2,400,384]{3,2,1,0:T(8,128)(2,1)S(1)}, bf16[8,2,400,384]{3,2,1,0:T(8,128)(2,1)}, u32[]{:S(2)}) copy-start(bf16[8,2,400,384]{3,2,1,0:T(8,128)(2,1)} %copy-done.1) | copy-start | bytes 14745604
  175.4 1.7 copy-start.5
  177.1 1.1 copy-start.7
  178.1 1.0 copy-start.22
  195.2 1.1 copy-start.20
  (17 other events, 14.3 us)
Sparse Core Ops, SparseCore 0:
  9.7 28.5 all-gather.2
  40.7 40.5 reduce-scatter.1

commit v3 on v2

v3 whole, which is shorter than its diff:
```python
import jax
import jax.numpy as jnp
from jax import lax
from jax.experimental import pallas as pl
from jax.experimental.pallas import tpu as pltpu
from jax.sharding import PartitionSpec as P

SIDE = 4
PARTS = ((0, 4), (4, 4), (8, 2), (10, 2), (12, 4))


def slot_of(d1, d2):
    low = d2 < 2
    return jnp.where(
        d1 == 0, 12 + d2,
        jnp.where(d1 == 1, jnp.where(low, 8 + d2, d2),
                  jnp.where(d1 == 2, jnp.where(low, d2, 2 + d2), jnp.where(low, 6 + d2, 8 + d2))))


def offsets(code):
    me = lax.axis_index("sx")
    dx = (code // SIDE - me // SIDE + SIDE) % SIDE
    dy = (code % SIDE - me % SIDE + SIDE) % SIDE
    return dx, dy


def left_kernel(partner_ref, counts_ref, own_ref, coupling_ref, left_ref, *rest):
    outs, (slots_y_ref, slots, used, sems) = rest[:10], rest[10:]
    t, step = pl.program_id(0), pl.program_id(1)
    last = pl.num_programs(1) - 1
    group = coupling_ref.shape[0]
    span = SIDE * SIDE
    span_y = slots.shape[0] - span
    modes, width = own_ref.shape

    @pl.when(step == 0)
    def _():
        for k in range(span + span_y):
            used[k] = 0

    for i in range(group):
        p = step * group + i
        keep = lax.broadcasted_iota(jnp.int32, (1, width), 1) < counts_ref[p]
        own = jnp.where(keep, own_ref[...], jnp.zeros((modes, width), own_ref.dtype))
        product = jnp.dot(own, coupling_ref[i, 0], preferred_element_type=jnp.float32)
        product = jnp.where(keep, product, 0.0).astype(jnp.bfloat16)
        left_ref[i, 0] = product

        code = partner_ref[p]
        dx, dy = offsets(code)
        slot = jnp.where(code < span, jnp.where(t == 0, slot_of(dx, dy), slot_of(dy, dx)), code)
        fresh = used[slot] == 0

        @pl.when(fresh)
        def _():
            slots[slot, t] = product
            used[slot] = 1

        @pl.when(jnp.logical_not(fresh))
        def _():
            slots[slot, t] = (slots[slot, t].astype(jnp.float32) + product.astype(jnp.float32)).astype(jnp.bfloat16)

    def copies(b):
        return [
            pltpu.make_async_copy(slots.at[pl.ds(at, size), b], outs[5 * b + i], sems.at[5 * b + i])
            for i, (at, size) in enumerate(PARTS)
        ]

    copy_y = pltpu.make_async_copy(slots.at[pl.ds(span, span_y)], slots_y_ref, sems.at[10])

    @pl.when(step == last)
    def _():
        @pl.loop(0, span + span_y)
        def _(k):
            @pl.when(used[k] == 0)
            def _():
                slots[k, t] = jnp.zeros((modes, width), slots.dtype)

        @pl.when(t == 0)
        def _():
            for c in copies(0):
                c.start()

        @pl.when(t == 1)
        def _():
            for c in copies(1):
                c.start()
            copy_y.start()
            for c in copies(0) + copies(1) + [copy_y]:
                c.wait()


def in_hbm(value):
    return pltpu.with_memory_space_constraint(value, pltpu.HBM)


def left_products(own, coupling, partner, counts, span_y):
    pairs, blocks, width, _ = coupling.shape
    modes = own.shape[0]
    group = 4
    piece = [pltpu.HBM((size, modes, width), jnp.bfloat16) for _, size in PARTS]
    anywhere = pl.BlockSpec(memory_space=pltpu.HBM)
    out = pl.pallas_call(
        left_kernel,
        grid_spec=pltpu.PrefetchScalarGridSpec(
            num_scalar_prefetch=2,
            grid=(blocks, pairs // group),
            in_specs=[
                pl.BlockSpec((modes, width), lambda t, p, *_: (0, 0)),
                pl.BlockSpec((group, 1, width, width), lambda t, p, *_: (p, t, 0, 0)),
            ],
            out_specs=[pl.BlockSpec((group, 1, modes, width), lambda t, p, *_: (p, t, 0, 0))] + [anywhere] * 11,
            scratch_shapes=[
                pltpu.VMEM((SIDE * SIDE + span_y, blocks, modes, width), jnp.bfloat16),
                pltpu.SMEM((SIDE * SIDE + span_y,), jnp.int32),
                pltpu.SemaphoreType.DMA((11,)),
            ],
        ),
        out_shape=[pltpu.HBM((pairs, blocks, modes, width), jnp.bfloat16)] + piece + piece
        + [pltpu.HBM((span_y, blocks, modes, width), jnp.bfloat16)],
        compiler_params=pltpu.CompilerParams(vmem_limit_bytes=26 * 2**20),
        cost_estimate=pl.CostEstimate(flops=2 * pairs * blocks * modes * width * width,
                                      bytes_accessed=25 * 10**6, transcendentals=0),
    )(partner, counts, in_hbm(own), in_hbm(coupling))
    return out[0], out[1:6], out[6:11], out[11]


def nt(a, b):
    return lax.dot_general(a, b, (((1,), (1,)), ((), ())), preferred_element_type=jnp.float32)


def pair_kernel(partner_ref, left_ref, *rest):
    halves, (ry_ref, out_ref, panels, sems) = (rest[:5], rest[5:10]), rest[10:]
    step = pl.program_id(0)
    group = out_ref.shape[0]
    pairs = panels.shape[0]
    span = SIDE * SIDE
    cut = halves[0][0].shape[1]
    rows = ((0, cut), (cut, panels.shape[1] - cut))

    @pl.when(step == 0)
    def _():
        @pl.loop(0, pairs)
        def _(q):
            code = partner_ref[q]
            dx, dy = offsets(code)

            @pl.when(code >= span)
            def _():
                for h, (at, size) in enumerate(rows):
                    pltpu.make_async_copy(ry_ref.at[code - span, pl.ds(at, size)], panels.at[q, pl.ds(at, size)],
                                          sems.at[q, h]).start()

            for h, (at, size) in enumerate(rows):
                d1, d2 = ((dx, dy), (dy, dx))[h]
                kept, near, far, low, high = halves[h]
                for ref, index, chosen in (
                    (kept, d1, d2 == 0), (near, d1, d2 == 1), (far, d1, d2 == 3),
                    (low, d1, (d2 == 2) & (d1 < 2)), (high, d1 - 2, (d2 == 2) & (d1 >= 2)),
                ):
                    @pl.when((code < span) & chosen)
                    def _():
                        pltpu.make_async_copy(ref.at[index], panels.at[q, pl.ds(at, size)], sems.at[q, h]).start()

    for i in range(group):
        p = step * group + i
        for h, (at, size) in enumerate(rows):
            pltpu.make_async_copy(ry_ref.at[0, pl.ds(at, size)], panels.at[p, pl.ds(at, size)], sems.at[p, h]).wait()
        for t in range(2):
            out_ref[i, t] = nt(left_ref[i, t], panels[p]).astype(jnp.bfloat16)


def pair_products(left, half_a, half_b, ry, partner):
    pairs, blocks, modes, width = left.shape
    group = 2
    anywhere = pl.BlockSpec(memory_space=pl.ANY)
    return pl.pallas_call(
        pair_kernel,
        grid_spec=pltpu.PrefetchScalarGridSpec(
            num_scalar_prefetch=1,
            grid=(pairs // group,),
            in_specs=[pl.BlockSpec((group, blocks, modes, width), lambda p, *_: (p, 0, 0, 0))] + [anywhere] * 10
            + [pl.BlockSpec(memory_space=pltpu.HBM)],
            out_specs=pl.BlockSpec((group, blocks, modes, modes), lambda p, *_: (p, 0, 0, 0)),
            scratch_shapes=[
                pltpu.VMEM((pairs, modes, width), jnp.bfloat16),
                pltpu.SemaphoreType.DMA((pairs, 2)),
            ],
        ),
        out_shape=jax.ShapeDtypeStruct((pairs, blocks, modes, modes), jnp.bfloat16),
        compiler_params=pltpu.CompilerParams(vmem_limit_bytes=16 * 2**20),
        cost_estimate=pl.CostEstimate(flops=2 * pairs * blocks * modes * width * modes,
                                      bytes_accessed=15 * 10**6, transcendentals=0),
    )(partner, in_hbm(left), *map(in_hbm, half_a), *map(in_hbm, half_b), in_hbm(ry))


def partner_kernel(own_ref, gy_ref, *rest):
    sums, out_ref = rest[:-1], rest[-1]
    each = len(sums) // 2
    for t in range(2):
        total = gy_ref[t].astype(jnp.float32)
        for ref in sums[t * each:(t + 1) * each]:
            total = total + ref[...].astype(jnp.float32)
        out_ref[t] = nt(own_ref[...], total.astype(jnp.bfloat16))


def partner_products(own, gy, sums):
    blocks, modes, width = gy.shape
    return pl.pallas_call(
        partner_kernel,
        out_shape=jax.ShapeDtypeStruct((blocks, modes, modes), jnp.float32),
        compiler_params=pltpu.CompilerParams(vmem_limit_bytes=16 * 2**20),
    )(*map(in_hbm, (own, gy, *sums)))


def shift(value, axis, by):
    moved = []
    for x in range(SIDE):
        for y in range(SIDE):
            to = ((x + by) % SIDE * SIDE + y) if axis == 0 else (x * SIDE + (y + by) % SIDE)
            moved.append((x * SIDE + y, to))
    return lax.ppermute(value, "sx", moved)


def after(value, *others):
    return lax.optimization_barrier((value,) + others)[0]


def added(*terms):
    return sum(v.astype(jnp.float32) for v in terms).astype(jnp.bfloat16)


def body(panels, coupling, partner, counts):
    own = jnp.swapaxes(panels[0], 0, 1)
    modes = own.shape[0]
    cut = (modes // 2 + 15) // 16 * 16
    ry = lax.all_gather(own, "sy", axis=0)

    pieces = (own[:cut], own[cut:])
    near = [[shift(pieces[h], h, -1), shift(pieces[h], h, 1)] for h in range(2)]
    opposite = [shift(pieces[h], h, 2) for h in range(2)]
    kept = [jnp.stack([pieces[h], near[h][0], opposite[h], near[h][1]]) for h in range(2)]

    kept = list(lax.optimization_barrier(tuple(kept)))

    ring = [[shift(kept[h], 1 - h, -1), shift(kept[h], 1 - h, 1)] for h in range(2)]
    left, parts0, parts1, slots_y = left_products(
        own, coupling, partner, after(counts, kept[0], kept[1]), lax.axis_size("sy")
    )
    sent, slots_y, ring = lax.optimization_barrier(
        ([[parts0[0], parts0[1]], [parts1[0], parts1[1]]], slots_y, ring)
    )
    gy = lax.psum_scatter(slots_y, "sy", scatter_dimension=0, tiled=True)

    parts = (parts0, parts1)
    got = [[shift(sent[t][0], t, 1), shift(sent[t][1], t, -1)] for t in range(2)]
    passed = []
    for h in range(2):
        low = shift(after(ring[h][0][:2], got[1 - h][1]), 1 - h, -1)
        high = shift(after(ring[h][1][2:], got[1 - h][0]), 1 - h, 1)
        passed.append([low, high])
    final = [
        [shift(added(parts[t][2], got[t][0][:2]), t, 1), shift(added(parts[t][3], got[t][1][:2]), t, -1)]
        for t in range(2)
    ]
    sums = []
    for t in range(2):
        here = parts[t][4]
        v = [
            added(here[0], got[t][1][2], final[t][0][0]),
            added(here[1], got[t][1][3], final[t][0][1]),
            added(here[2], got[t][0][2], final[t][1][0]),
            added(here[3], got[t][0][3], final[t][1][1]),
        ]
        sums.append(v)
    out = [[sums[t][0]] + [shift(sums[t][d], 1 - t, d) for d in (1, 3, 2)] for t in range(2)]

    halves = [[kept[h], *ring[h], *passed[h]] for h in range(2)]
    waits = [sums[t][d] for t in range(2) for d in (1, 2, 3)]
    pair_blocks = pair_products(left, halves[0], halves[1], ry, after(partner, *waits))
    partner_blocks = partner_products(own, gy[0], out[0] + out[1])
    return (pair_blocks, partner_blocks[None])


def solution(mesh):
    placed = (
        P(("sx", "sy"), None, None),
        P(("sx", "sy"), None, None, None),
        P(("sx", "sy")),
        P(("sx", "sy")),
    )
    return jax.shard_map(
        body,
        mesh=mesh,
        in_specs=placed,
        out_specs=(P(("sx", "sy"), None, None, None), P(("sx", "sy"), None, None, None)),
        check_vma=False,
    )
```

time: 210 us -> 142 us (0.68)
  waiting for transfers between devices: 88.3 us -> 51.1 us
  local copies, waits for them, and re-layouts: 30.7 us -> 4.7 us
  starting transfers between devices: 44.2 us -> 37.2 us
  Pallas kernels: 26.1 us -> 29.8 us
    ppermute x28, waiting for transfers between devices: 87.6 us -> 50.3 us  [shift(): return lax.ppermute(value, 'sx', moved)]
    unnamed x70 -> x50, local copies, waits for them, and re-layouts: 30.5 us -> 2.69 us
    ppermute x28, starting transfers between devices: 44.2 us -> 37.1 us  [shift(): return lax.ppermute(value, 'sx', moved)]
    pallas_call x1, Pallas kernels: 11.7 us -> 16.1 us  [left_products(): pl.pallas_call(left_kernel, grid_spec=pltpu.PrefetchScalarGridSpec(num_sc...]
  transfers between devices with their start and end apart: 30 -> 30, of which waited for: 11 -> 8; matrix products, arithmetic and copies ran while one was open for 2% -> 4% of each run, Pallas kernels for 11% -> 18%
where the time goes in v3:
time: 142 us; the launch traced here: 141 us
  waiting for transfers between devices  51.1 us (36%)
  starting transfers between devices  37.2 us (26%)
  Pallas kernels  29.8 us (21%)
  between operations  14.5 us (10%)
  local copies, waits for them, and re-layouts  4.7 us (3%)
  other arithmetic  3.61 us (3%)
    ppermute x28, waiting for transfers between devices, shift(): return lax.ppermute(value, 'sx', moved)  50.3 us
    ppermute x28, starting transfers between devices, shift(): return lax.ppermute(value, 'sx', moved)  37.1 us
    pallas_call x1, Pallas kernels, left_products(): pl.pallas_call(left_kernel, grid_spec=pltpu.PrefetchScalarGridSpec(num_sc...  16.1 us
    pallas_call x1, Pallas kernels, pair_products(): pl.pallas_call(pair_kernel, grid_spec=pltpu.PrefetchScalarGridSpec(num_sc...  9.97 us
    pallas_call x1, Pallas kernels, partner_products(): pl.pallas_call(partner_kernel, out_shape=jax.ShapeDtypeStruct((blocks, mo...  3.73 us
    convert_element_type x6, other arithmetic, added(): return sum((v.astype(jnp.float32) for v in terms)).astype(jnp.bfloat16)  3.42 us
  transfers between devices with their start and end apart: 30, of which 8 were waited for; matrix products, arithmetic and copies ran while one was open for 4% of the time, Pallas kernels for 18%

profile of v3, /device:TPU:0, one launch (start us, length us, event | category | flops | bytes accessed | tf_op | source)
XLA Modules:
  0.0 140.8 jit_solution(16350057331038058566)
XLA Ops:
  7.2 0.7 all-gather.3.cloned.1.call-update
  7.9 0.9 slice_bitcast_fusion
  8.9 1.7 %collective-permute-start.5 = (bf16[192,384]{1,0:T(8,128)(2,1)S(1)}, bf16[192,384]{1,0:T(8,128)(2,1)S(1)}, u32[]{:S(2)}, u32[]{:S(2)}) collective-permute-start(bf16[192,384]{1,0:T(8,128)(2,1)S(1)} %get-tuple-element.73), channel_id=1, source_target_pairs={{0,8},{8,16},{16,24},{24,0},{32,40},{40,48},{48,56},{56,32},{64,72... | collective-permute-start | bytes 442376 | tf_op jit(solution)/shard_map/ppermute | solution.py:222
  10.6 1.6 %collective-permute-start.3 = (bf16[192,384]{1,0:T(8,128)(2,1)S(1)}, bf16[192,384]{1,0:T(8,128)(2,1)S(1)}, u32[]{:S(2)}, u32[]{:S(2)}) collective-permute-start(bf16[192,384]{1,0:T(8,128)(2,1)S(1)} %get-tuple-element.73), channel_id=1, source_target_pairs={{0,24},{8,0},{16,8},{24,16},{32,56},{40,32},{48,40},{56,48},{64,88... | collective-permute-start | bytes 442376 | tf_op jit(solution)/shard_map/ppermute | solution.py:222
  12.2 2.1 %collective-permute-start.4 = (bf16[192,384]{1,0:T(8,128)(2,1)S(1)}, bf16[192,384]{1,0:T(8,128)(2,1)S(1)}, u32[]{:S(2)}, u32[]{:S(2)}) collective-permute-start(bf16[192,384]{1,0:T(8,128)(2,1)S(1)} %get-tuple-element.73), channel_id=1, source_target_pairs={{0,16},{8,24},{16,0},{24,8},{32,48},{40,56},{48,32},{56,40},{64,80... | collective-permute-start | bytes 442376 | tf_op jit(solution)/shard_map/ppermute | solution.py:222
  14.3 0.9 slice_bitcast_fusion.1
  15.2 2.8 %collective-permute-start = (bf16[208,384]{1,0:T(8,128)(2,1)S(1)}, bf16[208,384]{1,0:T(8,128)(2,1)S(1)}, u32[]{:S(2)}, u32[]{:S(2)}) collective-permute-start(bf16[208,384]{1,0:T(8,128)(2,1)S(1)} %get-tuple-element.75), channel_id=1, source_target_pairs={{0,96},{8,104},{16,112},{24,120},{32,0},{40,8},{48,16},{56,24},{64... | collective-permute-start | bytes 479240 | tf_op jit(solution)/shard_map/ppermute | solution.py:222
  18.0 0.8 collective-permute-start.1
  18.8 0.9 collective-permute-start.2
  19.7 0.5 collective-permute-done.4
  20.3 3.7 %collective-permute-done = bf16[208,384]{1,0:T(8,128)(2,1)S(1)} collective-permute-done((bf16[208,384]{1,0:T(8,128)(2,1)S(1)}, bf16[208,384]{1,0:T(8,128)(2,1)S(1)}, u32[]{:S(2)}, u32[]{:S(2)}) %collective-permute-start) | collective-permute-done | bytes 159776 | tf_op jit(solution)/shard_map/ppermute | solution.py:222
  24.0 2.0 %collective-permute-done.1 = bf16[208,384]{1,0:T(8,128)(2,1)S(1)} collective-permute-done((bf16[208,384]{1,0:T(8,128)(2,1)S(1)}, bf16[208,384]{1,0:T(8,128)(2,1)S(1)}, u32[]{:S(2)}, u32[]{:S(2)}) %collective-permute-start.1) | collective-permute-done | bytes 159776 | tf_op jit(solution)/shard_map/ppermute | solution.py:222
  26.0 1.7 %collective-permute-done.2 = bf16[208,384]{1,0:T(8,128)(2,1)S(1)} collective-permute-done((bf16[208,384]{1,0:T(8,128)(2,1)S(1)}, bf16[208,384]{1,0:T(8,128)(2,1)S(1)}, u32[]{:S(2)}, u32[]{:S(2)}) %collective-permute-start.2) | collective-permute-done | bytes 159776 | tf_op jit(solution)/shard_map/ppermute | solution.py:222
  27.8 1.1 collective-permute-start.6
  28.9 1.0 collective-permute-start.7
  29.9 0.6 collective-permute-start.8
  30.5 1.5 %collective-permute-start.9 = (bf16[4,192,384]{2,1,0:T(8,128)(2,1)S(1)}, bf16[4,192,384]{2,1,0:T(8,128)(2,1)S(1)}, u32[]{:S(2)}, u32[]{:S(2)}) collective-permute-start(bf16[4,192,384]{2,1,0:T(8,128)(2,1)S(1)} %pad_maximum_fusion.1.rest_5_), channel_id=1, source_target_pairs={{0,32},{8,40},{16,48},{24,56},{32,64},{40,72},{48,80},{56,88},{64,... | collective-permute-start | bytes 1769480 | tf_op jit(solution)/shard_map/ppermute | solution.py:222
  31.9 16.1 %shard_map.59 = (bf16[8,2,400,384]{3,2,1,0:T(8,128)(2,1)}, bf16[4,400,384]{2,1,0:T(8,128)(2,1)}, bf16[4,400,384]{2,1,0:T(8,128)(2,1)}, bf16[2,400,384]{2,1,0:T(8...) custom-call(s32[8]{0:T(128)S(1)} %copy-done, ...), custom_call_target="tpu_custom_call" | custom-call | flops 1887436800 | bytes 25000000 | tf_op jit(solution)/shard_map/pallas_call | solution.py:103
  48.1 0.8 copy-done.7
  49.0 2.4 %collective-permute-start.14 = (bf16[4,400,384]{2,1,0:T(8,128)(2,1)}, bf16[4,400,384]{2,1,0:T(8,128)(2,1)S(1)}, u32[]{:S(2)}, u32[]{:S(2)}) collective-permute-start(bf16[4,400,384]{2,1,0:T(8,128)(2,1)} %get-tuple-element.45), channel_id=1, source_target_pairs={{0,24},{8,0},{16,8},{24,16},{32,56},{40,32},{48,40},{56,48},{64,88... | collective-permute-start | bytes 3686408 | tf_op jit(solution)/shard_map/ppermute | solution.py:222
  51.3 1.4 %collective-permute-start.10 = (bf16[4,400,384]{2,1,0:T(8,128)(2,1)}, bf16[4,400,384]{2,1,0:T(8,128)(2,1)S(1)}, u32[]{:S(2)}, u32[]{:S(2)}) collective-permute-start(bf16[4,400,384]{2,1,0:T(8,128)(2,1)} %get-tuple-element.40), channel_id=1, source_target_pairs={{0,96},{8,104},{16,112},{24,120},{32,0},{40,8},{48,16},{56,24},{64... | collective-permute-start | bytes 3686408 | tf_op jit(solution)/shard_map/ppermute | solution.py:222
  52.8 0.6 collective-permute-start.11
  53.4 22.9 %collective-permute-done.14 = bf16[4,400,384]{2,1,0:T(8,128)(2,1)S(1)} collective-permute-done((bf16[4,400,384]{2,1,0:T(8,128)(2,1)}, bf16[4,400,384]{2,1,0:T(8,128)(2,1)S(1)}, u32[]{:S(2)}, u32[]{:S(2)}) %collective-permute-start.14) | collective-permute-done | bytes 1228832 | tf_op jit(solution)/shard_map/ppermute | solution.py:222
  76.2 0.2 add_convert_fusion
  76.4 3.5 %collective-permute-start.17 = (bf16[2,400,384]{2,1,0:T(8,128)(2,1)S(1)}, bf16[2,400,384]{2,1,0:T(8,128)(2,1)S(1)}, u32[]{:S(2)}, u32[]{:S(2)}) collective-permute-start(bf16[2,400,384]{2,1,0:T(8,128)(2,1)S(1)} %add_convert_fusion), channel_id=1, source_target_pairs={{0,24},{8,0},{16,8},{24,16},{32,56},{40,32},{48,40},{56,48},{64,88... | collective-permute-start | bytes 1843208 | tf_op jit(solution)/shard_map/ppermute | solution.py:222
  80.0 0.2 add_convert_fusion.1
  80.2 0.2 add_convert_fusion.2
  80.4 1.7 %collective-permute-start.13 = (bf16[2,400,384]{2,1,0:T(8,128)(2,1)S(1)}, bf16[2,400,384]{2,1,0:T(8,128)(2,1)S(1)}, u32[]{:S(2)}, u32[]{:S(2)}) collective-permute-start(bf16[2,400,384]{2,1,0:T(8,128)(2,1)S(1)} %add_convert_fusion.2), channel_id=1, source_target_pairs={{0,96},{8,104},{16,112},{24,120},{32,0},{40,8},{48,16},{56,24},{64... | collective-permute-start | bytes 1843208 | tf_op jit(solution)/shard_map/ppermute | solution.py:222
  82.1 0.2 add_convert_fusion.3
  82.3 0.5 collective-permute-start.12
  82.9 7.5 %collective-permute-done.17 = bf16[2,400,384]{2,1,0:T(8,128)(2,1)S(1)} collective-permute-done((bf16[2,400,384]{2,1,0:T(8,128)(2,1)S(1)}, bf16[2,400,384]{2,1,0:T(8,128)(2,1)S(1)}, u32[]{:S(2)}, u32[]{:S(2)}) %collective-permute-start.17) | collective-permute-done | bytes 614432 | tf_op jit(solution)/shard_map/ppermute | solution.py:222
  90.4 3.7 %collective-permute-start.18 = (bf16[2,208,384]{2,1,0:T(8,128)(2,1)S(1)}, bf16[2,208,384]{2,1,0:T(8,128)(2,1)S(1)}, u32[]{:S(2)}, u32[]{:S(2)}) collective-permute-start(bf16[2,208,384]{2,1,0:T(8,128)(2,1)S(1)} %slice.126), channel_id=1, source_target_pairs={{0,24},{8,0},{16,8},{24,16},{32,56},{40,32},{48,40},{56,48},{64,88... | collective-permute-start | bytes 958472 | tf_op jit(solution)/shard_map/ppermute | solution.py:222
  94.1 3.4 %collective-permute-done.16 = bf16[2,400,384]{2,1,0:T(8,128)(2,1)S(1)} collective-permute-done((bf16[2,400,384]{2,1,0:T(8,128)(2,1)S(1)}, bf16[2,400,384]{2,1,0:T(8,128)(2,1)S(1)}, u32[]{:S(2)}, u32[]{:S(2)}) %collective-permute-start.16) | collective-permute-done | bytes 614432 | tf_op jit(solution)/shard_map/ppermute | solution.py:222
  97.5 1.4 fusion.7
  98.9 0.9 collective-permute-start.25
  100.0 3.2 %collective-permute-start.20 = (bf16[2,192,384]{2,1,0:T(8,128)(2,1)S(1)}, bf16[2,192,384]{2,1,0:T(8,128)(2,1)S(1)}, u32[]{:S(2)}, u32[]{:S(2)}) collective-permute-start(bf16[2,192,384]{2,1,0:T(8,128)(2,1)S(1)} %slice.128), channel_id=1, source_target_pairs={{0,96},{8,104},{16,112},{24,120},{32,0},{40,8},{48,16},{56,24},{64... | collective-permute-start | bytes 884744 | tf_op jit(solution)/shard_map/ppermute | solution.py:222
  103.2 1.4 %fusion.6 = (bf16[400,384]{1,0:T(8,128)(2,1)}, bf16[400,384]{1,0:T(8,128)(2,1)}, bf16[400,384]{1,0:T(8,128)(2,1)S(1)}, bf16[400,384]{1,0:T(8,128)(2,1)S(1)}) fusion(bf16[2,400,384]{2,1,0:T(8,128)(2,1)S(1)} %collective-permute-done.12, bf16[4,400,384]{2,1,0:T(8,128)(2,1)S(1)} %collective-permute-done.10, bf16[4,400,384]{2,1,0:T(8,128)(2,1)S(1)} %copy-done.9, ...), kind=kLoop, calls=%fused_computation.20 | loop fusion | flops 3686400 | bytes 4915200 | tf_op jit(solution)/shard_map/convert_element_type | solution.py:230
  104.6 8.7 %collective-permute-done.21.rest_9_ = bf16[2,192,384]{2,1,0:T(8,128)(2,1)S(1)} collective-permute-done((bf16[2,192,384]{2,1,0:T(8,128)(2,1)S(1)}, bf16[2,192,384]{2,1,0:T(8,128)(2,1)S(1)}, u32[]{:S(2)}, u32[]{:S(2)}) %collective-permute-start.21) | collective-permute-done | bytes 294944 | tf_op jit(solution)/shard_map/ppermute | solution.py:222
  113.3 0.7 collective-permute-start.26
  114.0 1.1 collective-permute-start.27
  115.1 3.2 %collective-permute-start.23 = (bf16[400,384]{1,0:T(8,128)(2,1)S(1)}, bf16[400,384]{1,0:T(8,128)(2,1)S(1)}, u32[]{:S(2)}, u32[]{:S(2)}) collective-permute-start(bf16[400,384]{1,0:T(8,128)(2,1)S(1)} %get-tuple-element.71), channel_id=1, source_target_pairs={{0,24},{8,0},{16,8},{24,16},{32,56},{40,32},{48,40},{56,48},{64,88... | collective-permute-start | bytes 921608 | tf_op jit(solution)/shard_map/ppermute | solution.py:222
  118.3 0.7 copy-done.17
  119.1 10.0 %shard_map.60 = bf16[8,2,400,400]{3,2,1,0:T(8,128)(2,1)} custom-call(s32[8]{0:T(128)S(1)} %copy-done, bf16[8,2,400,384]{3,2,1,0:T(8,128)(2,1)} %get-tuple-element.50.left_ref, bf16[4,208,384]{2,1,0:T(8,128)(2,1)} %copy-done.2, bf16[4,208,384]{2,1,0:T(8,128)(2,1)} %copy-done.4, bf16[4,208,384]{2,1,0:T(8,128)(2,1)} %copy-done.5, ...), custom_call_target="tpu_custom_call" | custom-call | flops 1966080000 | bytes 15000000 | tf_op jit(solution)/shard_map/pallas_call | solution.py:177
  129.2 0.6 copy-done.18
  129.8 0.1 copy-done.19
  130.0 0.1 copy-done.21
  130.1 0.1 copy-done.22
  130.3 3.7 %shard_map.61 = f32[2,400,400]{2,1,0:T(8,128)} custom-call(bf16[400,384]{1,0:T(8,128)(2,1)} %bitcast.36, bf16[2,400,384]{2,1,0:T(8,128)(2,1)} %bitcast.39, bf16[400,384]{1,0:T(8,128)(2,1)} %get-tuple-element.62.rest_0_, bf16[400,384]{1,0:T(8,128)(2,1)} %copy-done.20, bf16[400,384]{1,0:T(8,128)(2,1)} %copy-done.21, bf16[400,384]{1,0:T(8,128)(2,1)} %copy-done.22, ...), custom_call_target="tpu_custom_call" | custom-call | tf_op jit(solution)/shard_map/pallas_call | solution.py:209
  (81 shorter events, 0.9 us)
Async XLA Ops:
  7.2 111.9 %all-gather.3.cloned.1.call-start = ((), (), s32[]{:S(2)}) async-start(), calls=%async_computation.2 | async-start | bytes 2764800 | tf_op jit(solution)/shard_map/all_gather | solution.py:237
  7.9 121.3 %reduce-scatter.2.cloned.1.call-start = ((), (), s32[]{:S(2)}) async-start(), calls=%async_computation.1 | async-start | bytes 5529600 | tf_op jit(solution)/shard_map/reduce_scatter | solution.py:253
  8.9 9.9 %collective-permute-start.5 = (bf16[192,384]{1,0:T(8,128)(2,1)S(1)}, bf16[192,384]{1,0:T(8,128)(2,1)S(1)}, u32[]{:S(2)}, u32[]{:S(2)}) collective-permute-start(bf16[192,384]{1,0:T(8,128)(2,1)S(1)} %get-tuple-element.73), channel_id=1, source_target_pairs={{0,8},{8,16},{16,24},{24,0},{32,40},{40,48},{48,56},{56,32},{64,72... | collective-permute-start | bytes 442376 | tf_op jit(solution)/shard_map/ppermute | solution.py:222
  10.6 9.1 %collective-permute-start.3 = (bf16[192,384]{1,0:T(8,128)(2,1)S(1)}, bf16[192,384]{1,0:T(8,128)(2,1)S(1)}, u32[]{:S(2)}, u32[]{:S(2)}) collective-permute-start(bf16[192,384]{1,0:T(8,128)(2,1)S(1)} %get-tuple-element.73), channel_id=1, source_target_pairs={{0,24},{8,0},{16,8},{24,16},{32,56},{40,32},{48,40},{56,48},{64,88... | collective-permute-start | bytes 442376 | tf_op jit(solution)/shard_map/ppermute | solution.py:222
  12.2 8.0 %collective-permute-start.4 = (bf16[192,384]{1,0:T(8,128)(2,1)S(1)}, bf16[192,384]{1,0:T(8,128)(2,1)S(1)}, u32[]{:S(2)}, u32[]{:S(2)}) collective-permute-start(bf16[192,384]{1,0:T(8,128)(2,1)S(1)} %get-tuple-element.73), channel_id=1, source_target_pairs={{0,16},{8,24},{16,0},{24,8},{32,48},{40,56},{48,32},{56,40},{64,80... | collective-permute-start | bytes 442376 | tf_op jit(solution)/shard_map/ppermute | solution.py:222
  15.2 8.8 %collective-permute-start = (bf16[208,384]{1,0:T(8,128)(2,1)S(1)}, bf16[208,384]{1,0:T(8,128)(2,1)S(1)}, u32[]{:S(2)}, u32[]{:S(2)}) collective-permute-start(bf16[208,384]{1,0:T(8,128)(2,1)S(1)} %get-tuple-element.75), channel_id=1, source_target_pairs={{0,96},{8,104},{16,112},{24,120},{32,0},{40,8},{48,16},{56,24},{64... | collective-permute-start | bytes 479240 | tf_op jit(solution)/shard_map/ppermute | solution.py:222
  18.0 8.0 %collective-permute-start.1 = (bf16[208,384]{1,0:T(8,128)(2,1)S(1)}, bf16[208,384]{1,0:T(8,128)(2,1)S(1)}, u32[]{:S(2)}, u32[]{:S(2)}) collective-permute-start(bf16[208,384]{1,0:T(8,128)(2,1)S(1)} %get-tuple-element.75), channel_id=1, source_target_pairs={{0,64},{8,72},{16,80},{24,88},{32,96},{40,104},{48,112},{56,120},{... | collective-permute-start | bytes 479240 | tf_op jit(solution)/shard_map/ppermute | solution.py:222
  18.8 8.9 %collective-permute-start.2 = (bf16[208,384]{1,0:T(8,128)(2,1)S(1)}, bf16[208,384]{1,0:T(8,128)(2,1)S(1)}, u32[]{:S(2)}, u32[]{:S(2)}) collective-permute-start(bf16[208,384]{1,0:T(8,128)(2,1)S(1)} %get-tuple-element.75), channel_id=1, source_target_pairs={{0,32},{8,40},{16,48},{24,56},{32,64},{40,72},{48,80},{56,88},{64,... | collective-permute-start | bytes 479240 | tf_op jit(solution)/shard_map/ppermute | solution.py:222
  20.2 11.7 %copy-start = (s32[8]{0:T(128)S(1)}, s32[8]{0:T(128)}, u32[]{:S(2)}) copy-start(s32[8]{0:T(128)} %partner_ref.2) | copy-start | bytes 100
  20.2 11.7 %copy-start.1 = (s32[8]{0:T(128)S(1)}, s32[8]{0:T(128)}, u32[]{:S(2)}) copy-start(s32[8]{0:T(128)} %counts_ref) | copy-start | bytes 100
  20.3 27.7 %copy-start.3 = (bf16[4,192,384]{2,1,0:T(8,128)(2,1)}, bf16[4,192,384]{2,1,0:T(8,128)(2,1)S(1)}, u32[]{:S(2)}) copy-start(bf16[4,192,384]{2,1,0:T(8,128)(2,1)S(1)} %pad_maximum_fusion.1.rest_5_) | copy-start | bytes 1769476
  27.8 20.2 %copy-start.2 = (bf16[4,208,384]{2,1,0:T(8,128)(2,1)}, bf16[4,208,384]{2,1,0:T(8,128)(2,1)S(1)}, u32[]{:S(2)}) copy-start(bf16[4,208,384]{2,1,0:T(8,128)(2,1)S(1)} %pad_maximum_fusion.rest_0_) | copy-start | bytes 1916932
  27.8 20.3 %collective-permute-start.6 = (bf16[4,208,384]{2,1,0:T(8,128)(2,1)S(1)}, bf16[4,208,384]{2,1,0:T(8,128)(2,1)S(1)}, u32[]{:S(2)}, u32[]{:S(2)}) collective-permute-start(bf16[4,208,384]{2,1,0:T(8,128)(2,1)S(1)} %pad_maximum_fusion.rest_0_), channel_id=1, source_target_pairs={{0,24},{8,0},{16,8},{24,16},{32,56},{40,32},{48,40},{56,48},{64,88... | collective-permute-start | bytes 1916936 | tf_op jit(solution)/shard_map/ppermute | solution.py:222
  28.9 19.2 %collective-permute-start.7 = (bf16[4,208,384]{2,1,0:T(8,128)(2,1)S(1)}, bf16[4,208,384]{2,1,0:T(8,128)(2,1)S(1)}, u32[]{:S(2)}, u32[]{:S(2)}) collective-permute-start(bf16[4,208,384]{2,1,0:T(8,128)(2,1)S(1)} %pad_maximum_fusion.rest_0_), channel_id=1, source_target_pairs={{0,8},{8,16},{16,24},{24,0},{32,40},{40,48},{48,56},{56,32},{64,72... | collective-permute-start | bytes 1916936 | tf_op jit(solution)/shard_map/ppermute | solution.py:222
  29.9 18.1 %collective-permute-start.8 = (bf16[4,192,384]{2,1,0:T(8,128)(2,1)S(1)}, bf16[4,192,384]{2,1,0:T(8,128)(2,1)S(1)}, u32[]{:S(2)}, u32[]{:S(2)}) collective-permute-start(bf16[4,192,384]{2,1,0:T(8,128)(2,1)S(1)} %pad_maximum_fusion.1.rest_5_), channel_id=1, source_target_pairs={{0,96},{8,104},{16,112},{24,120},{32,0},{40,8},{48,16},{56,24},{64... | collective-permute-start | bytes 1769480 | tf_op jit(solution)/shard_map/ppermute | solution.py:222
  30.5 17.6 %collective-permute-start.9 = (bf16[4,192,384]{2,1,0:T(8,128)(2,1)S(1)}, bf16[4,192,384]{2,1,0:T(8,128)(2,1)S(1)}, u32[]{:S(2)}, u32[]{:S(2)}) collective-permute-start(bf16[4,192,384]{2,1,0:T(8,128)(2,1)S(1)} %pad_maximum_fusion.1.rest_5_), channel_id=1, source_target_pairs={{0,32},{8,40},{16,48},{24,56},{32,64},{40,72},{48,80},{56,88},{64,... | collective-permute-start | bytes 1769480 | tf_op jit(solution)/shard_map/ppermute | solution.py:222
  48.0 51.8 %copy-start.6 = (bf16[4,192,384]{2,1,0:T(8,128)(2,1)}, bf16[4,192,384]{2,1,0:T(8,128)(2,1)S(1)}, u32[]{:S(2)}) copy-start(bf16[4,192,384]{2,1,0:T(8,128)(2,1)S(1)} %collective-permute-done.8.rest_6_) | copy-start | bytes 1769476
  48.1 34.7 %copy-start.4 = (bf16[4,208,384]{2,1,0:T(8,128)(2,1)}, bf16[4,208,384]{2,1,0:T(8,128)(2,1)S(1)}, u32[]{:S(2)}) copy-start(bf16[4,208,384]{2,1,0:T(8,128)(2,1)S(1)} %collective-permute-done.6.rest_1_) | copy-start | bytes 1916932
  48.9 33.8 %copy-start.5 = (bf16[4,208,384]{2,1,0:T(8,128)(2,1)}, bf16[4,208,384]{2,1,0:T(8,128)(2,1)S(1)}, u32[]{:S(2)}) copy-start(bf16[4,208,384]{2,1,0:T(8,128)(2,1)S(1)} %collective-permute-done.7.rest_2_) | copy-start | bytes 1916932
  48.9 27.3 %copy-start.14 = (bf16[2,400,384]{2,1,0:T(8,128)(2,1)S(1)}, bf16[2,400,384]{2,1,0:T(8,128)(2,1)}, u32[]{:S(2)}) copy-start(bf16[2,400,384]{2,1,0:T(8,128)(2,1)} %get-tuple-element.48) | copy-start | bytes 1843204
  48.9 31.0 %copy-start.13 = (bf16[2,400,384]{2,1,0:T(8,128)(2,1)S(1)}, bf16[2,400,384]{2,1,0:T(8,128)(2,1)}, u32[]{:S(2)}) copy-start(bf16[2,400,384]{2,1,0:T(8,128)(2,1)} %get-tuple-element.46) | copy-start | bytes 1843204
  49.0 27.3 %collective-permute-start.14 = (bf16[4,400,384]{2,1,0:T(8,128)(2,1)}, bf16[4,400,384]{2,1,0:T(8,128)(2,1)S(1)}, u32[]{:S(2)}, u32[]{:S(2)}) collective-permute-start(bf16[4,400,384]{2,1,0:T(8,128)(2,1)} %get-tuple-element.45), channel_id=1, source_target_pairs={{0,24},{8,0},{16,8},{24,16},{32,56},{40,32},{48,40},{56,48},{64,88... | collective-permute-start | bytes 3686408 | tf_op jit(solution)/shard_map/ppermute | solution.py:222
  51.3 28.6 %collective-permute-start.15 = (bf16[4,400,384]{2,1,0:T(8,128)(2,1)}, bf16[4,400,384]{2,1,0:T(8,128)(2,1)S(1)}, u32[]{:S(2)}, u32[]{:S(2)}) collective-permute-start(bf16[4,400,384]{2,1,0:T(8,128)(2,1)} %get-tuple-element.47), channel_id=1, source_target_pairs={{0,8},{8,16},{16,24},{24,0},{32,40},{40,48},{48,56},{56,32},{64,72... | collective-permute-start | bytes 3686408 | tf_op jit(solution)/shard_map/ppermute | solution.py:222
  51.3 28.9 %collective-permute-start.10 = (bf16[4,400,384]{2,1,0:T(8,128)(2,1)}, bf16[4,400,384]{2,1,0:T(8,128)(2,1)S(1)}, u32[]{:S(2)}, u32[]{:S(2)}) collective-permute-start(bf16[4,400,384]{2,1,0:T(8,128)(2,1)} %get-tuple-element.40), channel_id=1, source_target_pairs={{0,96},{8,104},{16,112},{24,120},{32,0},{40,8},{48,16},{56,24},{64... | collective-permute-start | bytes 3686408 | tf_op jit(solution)/shard_map/ppermute | solution.py:222
  52.8 29.4 %collective-permute-start.11 = (bf16[4,400,384]{2,1,0:T(8,128)(2,1)}, bf16[4,400,384]{2,1,0:T(8,128)(2,1)S(1)}, u32[]{:S(2)}, u32[]{:S(2)}) collective-permute-start(bf16[4,400,384]{2,1,0:T(8,128)(2,1)} %get-tuple-element.42), channel_id=1, source_target_pairs={{0,32},{8,40},{16,48},{24,56},{32,64},{40,72},{48,80},{56,88},{64,... | collective-permute-start | bytes 3686408 | tf_op jit(solution)/shard_map/ppermute | solution.py:222
  76.4 3.8 %copy-start.12 = (bf16[2,400,384]{2,1,0:T(8,128)(2,1)S(1)}, bf16[2,400,384]{2,1,0:T(8,128)(2,1)}, u32[]{:S(2)}) copy-start(bf16[2,400,384]{2,1,0:T(8,128)(2,1)} %get-tuple-element.43) | copy-start | bytes 1843204
  76.4 14.0 %collective-permute-start.17 = (bf16[2,400,384]{2,1,0:T(8,128)(2,1)S(1)}, bf16[2,400,384]{2,1,0:T(8,128)(2,1)S(1)}, u32[]{:S(2)}, u32[]{:S(2)}) collective-permute-start(bf16[2,400,384]{2,1,0:T(8,128)(2,1)S(1)} %add_convert_fusion), channel_id=1, source_target_pairs={{0,24},{8,0},{16,8},{24,16},{32,56},{40,32},{48,40},{56,48},{64,88... | collective-permute-start | bytes 1843208 | tf_op jit(solution)/shard_map/ppermute | solution.py:222
  80.1 2.0 %copy-start.11 = (bf16[2,400,384]{2,1,0:T(8,128)(2,1)S(1)}, bf16[2,400,384]{2,1,0:T(8,128)(2,1)}, u32[]{:S(2)}) copy-start(bf16[2,400,384]{2,1,0:T(8,128)(2,1)} %get-tuple-element.41) | copy-start | bytes 1843204
  80.1 17.4 %collective-permute-start.16 = (bf16[2,400,384]{2,1,0:T(8,128)(2,1)S(1)}, bf16[2,400,384]{2,1,0:T(8,128)(2,1)S(1)}, u32[]{:S(2)}, u32[]{:S(2)}) collective-permute-start(bf16[2,400,384]{2,1,0:T(8,128)(2,1)S(1)} %add_convert_fusion.1), channel_id=1, source_target_pairs={{0,8},{8,16},{16,24},{24,0},{32,40},{40,48},{48,56},{56,32},{64,72... | collective-permute-start | bytes 1843208 | tf_op jit(solution)/shard_map/ppermute | solution.py:222
  80.4 19.5 %collective-permute-start.13 = (bf16[2,400,384]{2,1,0:T(8,128)(2,1)S(1)}, bf16[2,400,384]{2,1,0:T(8,128)(2,1)S(1)}, u32[]{:S(2)}, u32[]{:S(2)}) collective-permute-start(bf16[2,400,384]{2,1,0:T(8,128)(2,1)S(1)} %add_convert_fusion.2), channel_id=1, source_target_pairs={{0,96},{8,104},{16,112},{24,120},{32,0},{40,8},{48,16},{56,24},{64... | collective-permute-start | bytes 1843208 | tf_op jit(solution)/shard_map/ppermute | solution.py:222
  82.1 15.4 %copy-start.10 = (bf16[4,400,384]{2,1,0:T(8,128)(2,1)S(1)}, bf16[4,400,384]{2,1,0:T(8,128)(2,1)}, u32[]{:S(2)}) copy-start(bf16[4,400,384]{2,1,0:T(8,128)(2,1)} %get-tuple-element.44) | copy-start | bytes 3686404
  82.3 17.7 %collective-permute-start.12 = (bf16[2,400,384]{2,1,0:T(8,128)(2,1)S(1)}, bf16[2,400,384]{2,1,0:T(8,128)(2,1)S(1)}, u32[]{:S(2)}, u32[]{:S(2)}) collective-permute-start(bf16[2,400,384]{2,1,0:T(8,128)(2,1)S(1)} %add_convert_fusion.3), channel_id=1, source_target_pairs={{0,32},{8,40},{16,48},{24,56},{32,64},{40,72},{48,80},{56,88},{64,... | collective-permute-start | bytes 1843208 | tf_op jit(solution)/shard_map/ppermute | solution.py:222
  82.8 32.2 %collective-permute-start.19 = (bf16[2,208,384]{2,1,0:T(8,128)(2,1)S(1)}, bf16[2,208,384]{2,1,0:T(8,128)(2,1)S(1)}, u32[]{:S(2)}, u32[]{:S(2)}) collective-permute-start(bf16[2,208,384]{2,1,0:T(8,128)(2,1)S(1)} %slice.127), channel_id=1, source_target_pairs={{0,8},{8,16},{16,24},{24,0},{32,40},{40,48},{48,56},{56,32},{64,72... | collective-permute-start | bytes 958472 | tf_op jit(solution)/shard_map/ppermute | solution.py:222
  90.4 24.6 %collective-permute-start.18 = (bf16[2,208,384]{2,1,0:T(8,128)(2,1)S(1)}, bf16[2,208,384]{2,1,0:T(8,128)(2,1)S(1)}, u32[]{:S(2)}, u32[]{:S(2)}) collective-permute-start(bf16[2,208,384]{2,1,0:T(8,128)(2,1)S(1)} %slice.126), channel_id=1, source_target_pairs={{0,24},{8,0},{16,8},{24,16},{32,56},{40,32},{48,40},{56,48},{64,88... | collective-permute-start | bytes 958472 | tf_op jit(solution)/shard_map/ppermute | solution.py:222
  97.5 2.3 %copy-start.8 = (bf16[4,192,384]{2,1,0:T(8,128)(2,1)S(1)}, bf16[4,192,384]{2,1,0:T(8,128)(2,1)}, u32[]{:S(2)}) copy-start(bf16[4,192,384]{2,1,0:T(8,128)(2,1)} %copy-done.7) | copy-start | bytes 1769476
  97.5 5.7 %copy-start.9 = (bf16[4,400,384]{2,1,0:T(8,128)(2,1)S(1)}, bf16[4,400,384]{2,1,0:T(8,128)(2,1)}, u32[]{:S(2)}) copy-start(bf16[4,400,384]{2,1,0:T(8,128)(2,1)} %get-tuple-element.34) | copy-start | bytes 3686404
  98.9 19.4 %collective-permute-start.25 = (bf16[400,384]{1,0:T(8,128)(2,1)S(1)}, bf16[400,384]{1,0:T(8,128)(2,1)S(1)}, u32[]{:S(2)}, u32[]{:S(2)}) collective-permute-start(bf16[400,384]{1,0:T(8,128)(2,1)S(1)} %get-tuple-element.61), channel_id=1, source_target_pairs={{0,32},{8,40},{16,48},{24,56},{32,64},{40,72},{48,80},{56,88},{64,... | collective-permute-start | bytes 921608 | tf_op jit(solution)/shard_map/ppermute | solution.py:222
  99.9 13.4 %collective-permute-start.21 = (bf16[2,192,384]{2,1,0:T(8,128)(2,1)S(1)}, bf16[2,192,384]{2,1,0:T(8,128)(2,1)S(1)}, u32[]{:S(2)}, u32[]{:S(2)}) collective-permute-start(bf16[2,192,384]{2,1,0:T(8,128)(2,1)S(1)} %slice.129), channel_id=1, source_target_pairs={{0,32},{8,40},{16,48},{24,56},{32,64},{40,72},{48,80},{56,88},{64,... | collective-permute-start | bytes 884744 | tf_op jit(solution)/shard_map/ppermute | solution.py:222
  100.0 14.0 %collective-permute-start.20 = (bf16[2,192,384]{2,1,0:T(8,128)(2,1)S(1)}, bf16[2,192,384]{2,1,0:T(8,128)(2,1)S(1)}, u32[]{:S(2)}, u32[]{:S(2)}) collective-permute-start(bf16[2,192,384]{2,1,0:T(8,128)(2,1)S(1)} %slice.128), channel_id=1, source_target_pairs={{0,96},{8,104},{16,112},{24,120},{32,0},{40,8},{48,16},{56,24},{64... | collective-permute-start | bytes 884744 | tf_op jit(solution)/shard_map/ppermute | solution.py:222
  113.3 5.8 %copy-start.23 = (bf16[2,192,384]{2,1,0:T(8,128)(2,1)}, bf16[2,192,384]{2,1,0:T(8,128)(2,1)S(1)}, u32[]{:S(2)}) copy-start(bf16[2,192,384]{2,1,0:T(8,128)(2,1)S(1)} %collective-permute-done.21.rest_9_) | copy-start | bytes 884740
  113.3 15.8 %collective-permute-start.26 = (bf16[400,384]{1,0:T(8,128)(2,1)}, bf16[400,384]{1,0:T(8,128)(2,1)S(1)}, u32[]{:S(2)}, u32[]{:S(2)}) collective-permute-start(bf16[400,384]{1,0:T(8,128)(2,1)} %get-tuple-element.69), channel_id=1, source_target_pairs={{0,96},{8,104},{16,112},{24,120},{32,0},{40,8},{48,16},{56,24},{64... | collective-permute-start | bytes 921608 | tf_op jit(solution)/shard_map/ppermute | solution.py:222
  114.0 5.1 %copy-start.24 = (bf16[2,192,384]{2,1,0:T(8,128)(2,1)}, bf16[2,192,384]{2,1,0:T(8,128)(2,1)S(1)}, u32[]{:S(2)}) copy-start(bf16[2,192,384]{2,1,0:T(8,128)(2,1)S(1)} %collective-permute-done.20.rest_8_) | copy-start | bytes 884740
  114.0 15.1 %collective-permute-start.27 = (bf16[400,384]{1,0:T(8,128)(2,1)}, bf16[400,384]{1,0:T(8,128)(2,1)S(1)}, u32[]{:S(2)}, u32[]{:S(2)}) collective-permute-start(bf16[400,384]{1,0:T(8,128)(2,1)} %get-tuple-element.68), channel_id=1, source_target_pairs={{0,64},{8,72},{16,80},{24,88},{32,96},{40,104},{48,112},{56,120},{... | collective-permute-start | bytes 921608 | tf_op jit(solution)/shard_map/ppermute | solution.py:222
  115.1 4.0 %copy-start.15 = (bf16[2,208,384]{2,1,0:T(8,128)(2,1)}, bf16[2,208,384]{2,1,0:T(8,128)(2,1)S(1)}, u32[]{:S(2)}) copy-start(bf16[2,208,384]{2,1,0:T(8,128)(2,1)S(1)} %collective-permute-done.19.rest_4_) | copy-start | bytes 958468
  115.1 14.1 %collective-permute-start.22 = (bf16[400,384]{1,0:T(8,128)(2,1)}, bf16[400,384]{1,0:T(8,128)(2,1)S(1)}, u32[]{:S(2)}, u32[]{:S(2)}) collective-permute-start(bf16[400,384]{1,0:T(8,128)(2,1)} %get-tuple-element.63), channel_id=1, source_target_pairs={{0,8},{8,16},{16,24},{24,0},{32,40},{40,48},{48,56},{56,32},{64,72... | collective-permute-start | bytes 921608 | tf_op jit(solution)/shard_map/ppermute | solution.py:222
  115.1 4.0 %copy-start.16 = (bf16[2,208,384]{2,1,0:T(8,128)(2,1)}, bf16[2,208,384]{2,1,0:T(8,128)(2,1)S(1)}, u32[]{:S(2)}) copy-start(bf16[2,208,384]{2,1,0:T(8,128)(2,1)S(1)} %collective-permute-done.18.rest_3_) | copy-start | bytes 958468
  115.1 14.1 %collective-permute-start.23 = (bf16[400,384]{1,0:T(8,128)(2,1)S(1)}, bf16[400,384]{1,0:T(8,128)(2,1)S(1)}, u32[]{:S(2)}, u32[]{:S(2)}) collective-permute-start(bf16[400,384]{1,0:T(8,128)(2,1)S(1)} %get-tuple-element.71), channel_id=1, source_target_pairs={{0,24},{8,0},{16,8},{24,16},{32,56},{40,32},{48,40},{56,48},{64,88... | collective-permute-start | bytes 921608 | tf_op jit(solution)/shard_map/ppermute | solution.py:222
  119.1 10.1 %collective-permute-start.24 = (bf16[400,384]{1,0:T(8,128)(2,1)S(1)}, bf16[400,384]{1,0:T(8,128)(2,1)S(1)}, u32[]{:S(2)}, u32[]{:S(2)}) collective-permute-start(bf16[400,384]{1,0:T(8,128)(2,1)S(1)} %get-tuple-element.70), channel_id=1, source_target_pairs={{0,16},{8,24},{16,0},{24,8},{32,48},{40,56},{48,32},{56,40},{64,80... | collective-permute-start | bytes 921608 | tf_op jit(solution)/shard_map/ppermute | solution.py:222
  (7 other events, 6.1 us)
Sparse Core Ops, SparseCore 0:
  9.7 28.4 all-gather.2
  49.1 40.1 reduce-scatter.1

commit v4 on v0

v4 whole, which is shorter than its diff:
```python
import jax
import jax.numpy as jnp
from jax import lax
from jax.experimental import pallas as pl
from jax.experimental.pallas import tpu as pltpu
from jax.sharding import PartitionSpec as P

SIDE = 4
SPAN_X, SPAN_Y = SIDE * SIDE, 2 * SIDE
PARTS = ((0, 4), (4, 4), (8, 2), (10, 2), (12, 4))
CHUNK = 80


def slot_of(d1, d2):
    if isinstance(d1, int):
        return {0: 12 + d2, 1: 8 + d2 if d2 < 2 else d2, 2: d2 if d2 < 2 else 2 + d2, 3: 6 + d2 if d2 < 2 else 8 + d2}[d1]
    low = d2 < 2
    return jnp.where(
        d1 == 0, 12 + d2,
        jnp.where(d1 == 1, jnp.where(low, 8 + d2, d2),
                  jnp.where(d1 == 2, jnp.where(low, d2, 2 + d2), jnp.where(low, 6 + d2, 8 + d2))))


def place_of(slot):
    for n, (at, size) in enumerate(PARTS):
        if at <= slot < at + size:
            return n, slot - at


def offsets(code):
    me = lax.axis_index("sx")
    dx = (code // SIDE - me // SIDE + SIDE) % SIDE
    dy = (code % SIDE - me % SIDE + SIDE) % SIDE
    return dx, dy


def ring_offset(code):
    me = lax.axis_index("sy")
    other = code - SPAN_X
    return (other // 2 - me // 2 + SIDE) % SIDE, other % 2, me % 2


def left_kernel(partner_ref, counts_ref, own_hbm, coupling_hbm, left_hbm, *rest):
    first, second, (z_other, z_mine) = rest[:5], rest[5:10], rest[10:12]
    own_ref, blocks, lefts, slots, used, in_sem, left_sem, out_sem = rest[12:]
    count = blocks.shape[0]
    modes, width = own_ref.shape
    cut = first[0].shape[2]

    def load(i):
        return pltpu.make_async_copy(coupling_hbm.at[i // 2, i % 2], blocks.at[i], in_sem.at[i])

    def save(i):
        return pltpu.make_async_copy(lefts.at[i], left_hbm.at[i // 2, i % 2], left_sem.at[i])

    load_own = pltpu.make_async_copy(own_hbm, own_ref, in_sem.at[count])
    load_own.start()

    @pl.loop(0, count)
    def _(i):
        load(i).start()

    @pl.loop(0, SPAN_X + SPAN_Y)
    def _(k):
        used[k] = 0

    load_own.wait()

    @pl.loop(0, count)
    def _(i):
        p, t = i // 2, i % 2
        load(i).wait()
        keep = lax.broadcasted_iota(jnp.int32, (1, width), 1) < counts_ref[p]
        own = jnp.where(keep, own_ref[...], jnp.zeros((modes, width), own_ref.dtype))
        product = jnp.dot(own, blocks[i], preferred_element_type=jnp.float32)
        lefts[i] = jnp.where(keep, product, 0.0).astype(jnp.bfloat16)
        save(i).start()

        code = partner_ref[p]
        dx, dy = offsets(code)
        dz, core, me = ring_offset(code)
        turn = jnp.where((dz == 1) | (dz == 3), jnp.where((dz == 1) == (core == 0), 1, 2), jnp.where(dz == 2, 3, 0))
        slot = jnp.where(code < SPAN_X, slot_of(dx, dy), SPAN_X + turn + jnp.where(core == me, SIDE, 0))
        fresh = (used[slot] == 0) | (used[slot] == p + 1)

        @pl.when(fresh)
        def _():
            used[slot] = p + 1

        @pl.loop(0, modes // CHUNK)
        def _(r):
            rows = pl.ds(pl.multiple_of(r * CHUNK, CHUNK), CHUNK)
            before = jnp.where(fresh, 0.0, slots[slot, t, rows].astype(jnp.float32))
            slots[slot, t, rows] = (before + lefts[i, rows].astype(jnp.float32)).astype(jnp.bfloat16)

    @pl.loop(0, SPAN_X + SPAN_Y)
    def _(k):
        @pl.when(used[k] == 0)
        def _():
            @pl.loop(0, 2 * (modes // CHUNK))
            def _(r):
                rows = pl.ds(pl.multiple_of(r // 2 * CHUNK, CHUNK), CHUNK)
                slots[k, r % 2, rows] = jnp.zeros((CHUNK, width), slots.dtype)

    copies = [
        pltpu.make_async_copy(slots.at[pl.ds(at, size), :, pl.ds(0, cut)], first[n], out_sem.at[n])
        for n, (at, size) in enumerate(PARTS)
    ]
    copies.append(pltpu.make_async_copy(slots.at[pl.ds(SPAN_X, SIDE)], z_other, out_sem.at[5]))
    copies.append(pltpu.make_async_copy(slots.at[pl.ds(SPAN_X + SIDE, SIDE)], z_mine, out_sem.at[6]))
    for dx in range(SIDE):
        for dy in range(SIDE):
            n, at = place_of(slot_of(dy, dx))
            copies.append(pltpu.make_async_copy(
                slots.at[slot_of(dx, dy), :, pl.ds(cut, modes - cut)], second[n].at[at], out_sem.at[7 + dx * SIDE + dy]))
    for c in copies:
        c.start()

    @pl.loop(0, count)
    def _(i):
        save(i).wait()

    for c in copies:
        c.wait()


def in_hbm(value):
    return pltpu.with_memory_space_constraint(value, pltpu.HBM)


def left_products(own, coupling, partner, counts, cut):
    pairs, blocks, width, _ = coupling.shape
    modes = own.shape[0]
    hbm, smem = pl.BlockSpec(memory_space=pltpu.HBM), pl.BlockSpec(memory_space=pltpu.SMEM)
    shapes = [(pairs, blocks, modes, width)]
    shapes += [(size, blocks, cut, width) for _, size in PARTS]
    shapes += [(size, blocks, modes - cut, width) for _, size in PARTS]
    shapes += [(SIDE, blocks, modes, width)] * 2
    out = pl.pallas_call(
        left_kernel,
        in_specs=[smem, smem, hbm, hbm],
        out_specs=[hbm] * len(shapes),
        out_shape=[pltpu.HBM(s, jnp.bfloat16) for s in shapes],
        scratch_shapes=[
            pltpu.VMEM((modes, width), jnp.bfloat16),
            pltpu.VMEM((pairs * blocks, width, width), jnp.bfloat16),
            pltpu.VMEM((pairs * blocks, modes, width), jnp.bfloat16),
            pltpu.VMEM((SPAN_X + SPAN_Y, blocks, modes, width), jnp.bfloat16),
            pltpu.SMEM((SPAN_X + SPAN_Y,), jnp.int32),
            pltpu.SemaphoreType.DMA((pairs * blocks + 1,)),
            pltpu.SemaphoreType.DMA((pairs * blocks,)),
            pltpu.SemaphoreType.DMA((7 + SPAN_X,)),
        ],
        compiler_params=pltpu.CompilerParams(vmem_limit_bytes=32 * 2**20),
        cost_estimate=pl.CostEstimate(flops=2 * pairs * blocks * modes * width * width,
                                      bytes_accessed=25 * 10**6, transcendentals=0),
    )(partner, counts, in_hbm(own), in_hbm(coupling))
    return out[0], out[1:6], out[6:11], out[11], out[12]


def nt(a, b):
    return lax.dot_general(a, b, (((1,), (1,)), ((), ())), preferred_element_type=jnp.float32)


def pair_kernel(partner_ref, left_hbm, *rest):
    (kept, near, far, low, high, ring_mine, ring_other), out_hbm = rest[:7], rest[7]
    lefts, panels, outs, left_sem, panel_sem, out_sem = rest[8:]
    pairs, count = panels.shape[0], lefts.shape[0]

    def load(i):
        return pltpu.make_async_copy(left_hbm.at[i // 2, i % 2], lefts.at[i], left_sem.at[i])

    def save(i):
        return pltpu.make_async_copy(outs.at[i], out_hbm.at[i // 2, i % 2], out_sem.at[i])

    @pl.loop(0, pairs)
    def _(q):
        load(2 * q).start()
        load(2 * q + 1).start()
        code = partner_ref[q]
        dx, dy = offsets(code)
        dz, core, me = ring_offset(code)
        turn = jnp.where((dz == 1) | (dz == 3), jnp.where((dz == 3) == (core == 0), 1, 2), jnp.where(dz == 2, 3, 0))
        along = code < SPAN_X
        for ref, index, chosen in (
            (kept, dx, along & (dy == 0)),
            (near, dx, along & (dy == 1)),
            (far, dx, along & (dy == 3)),
            (low, dx, along & (dy == 2) & (dx < 2)),
            (high, dx - 2, along & (dy == 2) & (dx >= 2)),
            (ring_mine, turn, (code >= SPAN_X) & (core == me)),
            (ring_other, turn, (code >= SPAN_X) & (core != me)),
        ):
            @pl.when(chosen)
            def _():
                pltpu.make_async_copy(ref.at[index], panels.at[q], panel_sem.at[q]).start()

    @pl.loop(0, count)
    def _(i):
        p = i // 2

        @pl.when(i % 2 == 0)
        def _():
            pltpu.make_async_copy(kept.at[0], panels.at[p], panel_sem.at[p]).wait()

        load(i).wait()
        outs[i] = nt(lefts[i], panels[p]).astype(jnp.bfloat16)
        save(i).start()

    @pl.loop(0, count)
    def _(i):
        save(i).wait()


def pair_products(left, sources, partner):
    pairs, blocks, modes, width = left.shape
    hbm, smem = pl.BlockSpec(memory_space=pltpu.HBM), pl.BlockSpec(memory_space=pltpu.SMEM)
    return pl.pallas_call(
        pair_kernel,
        in_specs=[smem] + [hbm] * 8,
        out_specs=hbm,
        out_shape=jax.ShapeDtypeStruct((pairs, blocks, modes, modes), jnp.bfloat16),
        scratch_shapes=[
            pltpu.VMEM((pairs * blocks, modes, width), jnp.bfloat16),
            pltpu.VMEM((pairs, modes, width), jnp.bfloat16),
            pltpu.VMEM((pairs * blocks, modes, modes), jnp.bfloat16),
            pltpu.SemaphoreType.DMA((pairs * blocks,)),
            pltpu.SemaphoreType.DMA((pairs,)),
            pltpu.SemaphoreType.DMA((pairs * blocks,)),
        ],
        compiler_params=pltpu.CompilerParams(vmem_limit_bytes=20 * 2**20),
        cost_estimate=pl.CostEstimate(flops=2 * pairs * blocks * modes * width * modes,
                                      bytes_accessed=15 * 10**6, transcendentals=0),
    )(partner, in_hbm(left), *map(in_hbm, sources))


def partner_kernel(own_ref, top_ref, bottom_ref, *rest):
    last, out_ref, total = rest[:3], rest[3], rest[4]
    cut = top_ref.shape[1]

    @pl.loop(0, out_ref.shape[0])
    def _(t):
        top = top_ref[t]
        for ref in last:
            top = top + ref[t].astype(jnp.float32)
        total[:cut] = top.astype(jnp.bfloat16)
        total[cut:] = bottom_ref[t].astype(jnp.bfloat16)
        out_ref[t] = nt(own_ref[...], total[...])


def partner_products(own, top, bottom, last):
    modes, width = own.shape
    blocks = top.shape[0]
    return pl.pallas_call(
        partner_kernel,
        out_shape=jax.ShapeDtypeStruct((blocks, modes, modes), jnp.float32),
        scratch_shapes=[pltpu.VMEM((modes, width), jnp.bfloat16)],
        compiler_params=pltpu.CompilerParams(vmem_limit_bytes=16 * 2**20),
    )(own, top, bottom, *last)


def shift(value, axis, by):
    moved = []
    for x in range(SIDE):
        for y in range(SIDE):
            to = ((x + by) % SIDE * SIDE + y) if axis == 0 else (x * SIDE + (y + by) % SIDE)
            moved.append((x * SIDE + y, to))
    return lax.ppermute(value, "sx", moved)


def turn(value, by):
    moved = [(2 * z + c, (z + (by if c == 0 else -by)) % SIDE * 2 + c) for z in range(SIDE) for c in range(2)]
    return lax.ppermute(value, "sy", moved)


def swap(value):
    return lax.ppermute(value, "sy", [(2 * z + c, 2 * z + 1 - c) for z in range(SIDE) for c in range(2)])


def added(*terms):
    return sum(v.astype(jnp.float32) for v in terms)


def rounded(*terms):
    return added(*terms).astype(jnp.bfloat16)


def settled(parts, got, last):
    here = parts[4]
    return [
        rounded(here[0], got[1][2], last[0][0]),
        rounded(here[1], got[1][3], last[0][1]),
        rounded(here[2], got[0][2], last[1][0]),
        rounded(here[3], got[0][3], last[1][1]),
    ]


def body(panels, coupling, partner, counts):
    own = jnp.swapaxes(panels[0], 0, 1)
    cut = -(-own.shape[0] * 3 // 64) * 16
    barrier = lax.optimization_barrier

    x1, x3, x2 = shift(own, 0, -1), shift(own, 0, 1), shift(own, 0, 2)
    ring = jnp.stack([own, turn(own, 1), turn(own, -1), turn(own, 2)])
    kept = jnp.stack([own, x1, x2, x3])
    left, top, bottom, z_other, z_mine = left_products(own, coupling, partner, counts, cut)

    kept, up, down = barrier((kept, top[0], top[1]))
    near, far = shift(kept, 1, -1), shift(kept, 1, 1)
    got = [shift(up, 0, 1), shift(down, 0, -1)]

    z_other, ring = barrier((z_other, ring))
    ring_other = swap(ring)
    pair_sum = swap(z_other)
    w = [rounded(z_mine[k], pair_sum[k]) for k in range(SIDE)]
    z_sum = added(w[0], turn(w[1], 1), turn(w[2], -1), turn(w[3], 2))

    near, far, up, down = barrier((near, far, bottom[0], bottom[1]))
    got_b = [shift(up, 1, 1), shift(down, 1, -1)]
    near, far, got_b = barrier((near, far, got_b))
    low, high = shift(near[:2], 1, -1), shift(far[2:], 1, 1)
    pass_b = [rounded(bottom[2], got_b[0][:2]), rounded(bottom[3], got_b[1][:2])]
    pass_b, low, high = barrier((pass_b, low, high))
    last_b = [shift(pass_b[0], 1, 1), shift(pass_b[1], 1, -1)]

    last = [shift(rounded(top[2], got[0][:2]), 0, 1), shift(rounded(top[3], got[1][:2]), 0, -1)]
    v = settled(top, got, last)
    v_b = settled(bottom, got_b, last_b)
    ends = [shift(v[1], 1, 1), shift(v[3], 1, -1), shift(v[2], 1, 2)]
    ends_b = [shift(v_b[1], 0, 1), shift(v_b[3], 0, -1), shift(v_b[2], 0, 2)]

    sources = [kept, near, far, low, high, ring, ring_other]
    pair_blocks = pair_products(left, sources, barrier((partner, v))[0])
    partner_blocks = partner_products(
        own, added(v[0], z_sum[:, :cut]), added(v_b[0], *ends_b, z_sum[:, cut:]), ends
    )
    return (pair_blocks, partner_blocks[None])


def solution(mesh):
    placed = (
        P(("sx", "sy"), None, None),
        P(("sx", "sy"), None, None, None),
        P(("sx", "sy")),
        P(("sx", "sy")),
    )
    return jax.shard_map(
        body,
        mesh=mesh,
        in_specs=placed,
        out_specs=(P(("sx", "sy"), None, None, None), P(("sx", "sy"), None, None, None)),
        check_vma=False,
    )
```

time: 309 us -> 151 us (0.49)
  the two profiles are of different devices: /device:TPU:0 before, /device:TPU:31 now
where the time goes in v4:
time: 151 us
  waiting for transfers between devices  77.7 us (51%)
  starting transfers between devices  37.1 us (25%)
  Pallas kernels  29.9 us (20%)
  other arithmetic  2.99 us (2%)
  local copies, waits for them, and re-layouts  2.33 us (2%)
    ppermute x21, waiting for transfers between devices, shift(): return lax.ppermute(value, 'sx', moved)  58.9 us
    ppermute x21, starting transfers between devices, shift(): return lax.ppermute(value, 'sx', moved)  21.1 us
    ppermute x6, waiting for transfers between devices, turn(): return lax.ppermute(value, 'sy', moved)  18.8 us
    pallas_call x1, Pallas kernels, left_products(): pl.pallas_call(left_kernel, in_specs=[smem, smem, hbm, hbm], out_specs=[h...  18.6 us
    ppermute x6, starting transfers between devices, turn(): return lax.ppermute(value, 'sy', moved)  10.9 us
    pallas_call x1, Pallas kernels, pair_products(): pl.pallas_call(pair_kernel, in_specs=[smem] + [hbm] * 8, out_specs=hbm, o...  9.21 us
    ppermute x2, starting transfers between devices, swap(): lax.ppermute(value, 'sy', [(2 * z + c, 2 * z + 1 - c) for z in range(SIDE...  5.12 us
  transfers between devices with their start and end apart: 29, of which 9 were waited for; matrix products, arithmetic and copies ran while one was open for 2% of the time, Pallas kernels for 18%

profile of v4, /device:TPU:31, one launch (start us, length us, event | category | flops | bytes accessed | tf_op | source)
XLA Modules:
  0.0 151.0 jit_solution(588363755791913976)
XLA Ops:
  0.6 0.3 collective-permute-start.2
  0.9 2.1 %collective-permute-start.1 = (bf16[400,384]{1,0:T(8,128)(2,1)}, bf16[400,384]{1,0:T(8,128)(2,1)S(1)}, u32[]{:S(2)}, u32[]{:S(2)}) collective-permute-start(bf16[400,384]{1,0:T(8,128)(2,1)} %bitcast.44), channel_id=1, source_target_pairs={{0,64},{8,72},{16,80},{24,88},{32,96},{40,104},{48,112},{56,120},{... | collective-permute-start | bytes 921608 | tf_op jit(solution)/shard_map/ppermute | solution.py:268
  3.1 3.6 %collective-permute-start.15 = (bf16[400,384]{1,0:T(8,128)(2,1)}, bf16[400,384]{1,0:T(8,128)(2,1)S(1)}, u32[]{:S(2)}, u32[]{:S(2)}) collective-permute-start(bf16[400,384]{1,0:T(8,128)(2,1)} %bitcast.46), channel_id=1, source_target_pairs={{0,4},{1,5},{2,6},{3,7},{4,0},{5,1},{6,2},{7,3},{8,12},{9,13},{10,... | collective-permute-start | bytes 921608 | tf_op jit(solution)/shard_map/ppermute | solution.py:273
  6.6 0.7 collective-permute-start.14
  7.4 1.7 %collective-permute-done.2 = bf16[400,384]{1,0:T(8,128)(2,1)S(1)} collective-permute-done((bf16[400,384]{1,0:T(8,128)(2,1)}, bf16[400,384]{1,0:T(8,128)(2,1)S(1)}, u32[]{:S(2)}, u32[]{:S(2)}) %collective-permute-start.2) | collective-permute-done | bytes 307232 | tf_op jit(solution)/shard_map/ppermute | solution.py:268
  9.1 3.8 %collective-permute-start.13 = (bf16[400,384]{1,0:T(8,128)(2,1)}, bf16[400,384]{1,0:T(8,128)(2,1)S(1)}, u32[]{:S(2)}, u32[]{:S(2)}) collective-permute-start(bf16[400,384]{1,0:T(8,128)(2,1)} %bitcast.48), channel_id=1, source_target_pairs={{0,2},{1,7},{2,4},{3,1},{4,6},{5,3},{6,0},{7,5},{8,10},{9,15},{10,... | collective-permute-start | bytes 921608 | tf_op jit(solution)/shard_map/ppermute | solution.py:273
  12.8 0.7 copy-done.1
  13.5 0.7 copy-done.2
  14.1 18.6 %shard_map.59 = (bf16[8,2,400,384]{3,2,1,0:T(8,128)(2,1)}, bf16[4,2,304,384]{3,2,1,0:T(8,128)(2,1)}, bf16[4,2,304,384]{3,2,1,0:T(8,128)(2,1)}, bf16[2,2,304,384]...) custom-call(s32[8]{0:T(128)S(1)} %copy-done.1, ...), custom_call_target="tpu_custom_call" | custom-call | flops 1887436800 | bytes 25000000 | tf_op jit(solution)/shard_map/pallas_call | solution.py:139
  32.9 0.4 fusion.1
  33.3 1.6 %collective-permute-start.4 = (bf16[4,2,304,384]{3,2,1,0:T(8,128)(2,1)}, bf16[4,2,304,384]{3,2,1,0:T(8,128)(2,1)S(1)}, u32[]{:S(2)}, u32[]{:S(2)}) collective-permute-start(bf16[4,2,304,384]{3,2,1,0:T(8,128)(2,1)} %get-tuple-element.38), channel_id=1, source_target_pairs={{0,32},{8,40},{16,48},{24,56},{32,64},{40,72},{48,80},{56,88},{64,... | collective-permute-start | bytes 5603336 | tf_op jit(solution)/shard_map/ppermute | solution.py:268
  34.9 0.5 collective-permute-start.7
  35.4 2.2 %collective-permute-start.8 = (bf16[4,400,384]{2,1,0:T(8,128)(2,1)S(1)}, bf16[4,400,384]{2,1,0:T(8,128)(2,1)S(1)}, u32[]{:S(2)}, u32[]{:S(2)}) collective-permute-start(bf16[4,400,384]{2,1,0:T(8,128)(2,1)S(1)} %get-tuple-element.42.rest_0_), channel_id=1, source_target_pairs={{0,8},{8,16},{16,24},{24,0},{32,40},{40,48},{48,56},{56,32},{64,72... | collective-permute-start | bytes 3686408 | tf_op jit(solution)/shard_map/ppermute | solution.py:268
  37.6 1.7 %collective-permute-start.17 = (bf16[4,2,400,384]{3,2,1,0:T(8,128)(2,1)S(1)}, bf16[4,2,400,384]{3,2,1,0:T(8,128)(2,1)S(1)}, u32[]{:S(2)}, u32[]{:S(2)}) collective-permute-start(bf16[4,2,400,384]{3,2,1,0:T(8,128)(2,1)S(1)} %copy-done.17), channel_id=1, source_target_pairs={{0,1},{1,0},{2,3},{3,2},{4,5},{5,4},{6,7},{7,6},{8,9},{9,8},{10,11... | collective-permute-start | bytes 7372808 | tf_op jit(solution)/shard_map/ppermute | solution.py:277
  39.3 25.5 %collective-permute-done.7.rest_1_ = bf16[4,400,384]{2,1,0:T(8,128)(2,1)S(1)} collective-permute-done((bf16[4,400,384]{2,1,0:T(8,128)(2,1)S(1)}, bf16[4,400,384]{2,1,0:T(8,128)(2,1)S(1)}, u32[]{:S(2)}, u32[]{:S(2)}) %collective-permute-start.7) | collective-permute-done | bytes 1228832 | tf_op jit(solution)/shard_map/ppermute | solution.py:268
  64.8 2.3 %collective-permute-start.9 = (bf16[4,2,96,384]{3,2,1,0:T(8,128)(2,1)}, bf16[4,2,96,384]{3,2,1,0:T(8,128)(2,1)S(1)}, u32[]{:S(2)}, u32[]{:S(2)}) collective-permute-start(bf16[4,2,96,384]{3,2,1,0:T(8,128)(2,1)} %get-tuple-element.47), channel_id=1, source_target_pairs={{0,8},{8,16},{16,24},{24,0},{32,40},{40,48},{48,56},{56,32},{64,72... | collective-permute-start | bytes 1769480 | tf_op jit(solution)/shard_map/ppermute | solution.py:268
  67.1 12.0 %collective-permute-done.9 = bf16[4,2,96,384]{3,2,1,0:T(8,128)(2,1)S(1)} collective-permute-done((bf16[4,2,96,384]{3,2,1,0:T(8,128)(2,1)}, bf16[4,2,96,384]{3,2,1,0:T(8,128)(2,1)S(1)}, u32[]{:S(2)}, u32[]{:S(2)}) %collective-permute-start.9) | collective-permute-done | bytes 589856 | tf_op jit(solution)/shard_map/ppermute | solution.py:268
  79.2 2.8 %collective-permute-done.10 = bf16[4,2,96,384]{3,2,1,0:T(8,128)(2,1)S(1)} collective-permute-done((bf16[4,2,96,384]{3,2,1,0:T(8,128)(2,1)}, bf16[4,2,96,384]{3,2,1,0:T(8,128)(2,1)S(1)}, u32[]{:S(2)}, u32[]{:S(2)}) %collective-permute-start.10) | collective-permute-done | bytes 589856 | tf_op jit(solution)/shard_map/ppermute | solution.py:268
  82.1 0.1 collective-permute-start.11
  82.2 2.7 %collective-permute-start.12 = (bf16[2,400,384]{2,1,0:T(8,128)(2,1)S(1)}, bf16[2,400,384]{2,1,0:T(8,128)(2,1)S(1)}, u32[]{:S(2)}, u32[]{:S(2)}) collective-permute-start(bf16[2,400,384]{2,1,0:T(8,128)(2,1)S(1)} %slice.137), channel_id=1, source_target_pairs={{0,8},{8,16},{16,24},{24,0},{32,40},{40,48},{48,56},{56,32},{64,72... | collective-permute-start | bytes 1843208 | tf_op jit(solution)/shard_map/ppermute | solution.py:268
  85.0 0.3 add_convert_fusion.1
  85.2 0.1 collective-permute-start.5
  85.3 0.8 copy-done.10
  86.2 0.3 add_convert_fusion
  86.4 0.7 collective-permute-start.6
  87.1 0.2 add_convert_fusion.10
  87.3 9.1 %collective-permute-done.11.rest_3_ = bf16[2,400,384]{2,1,0:T(8,128)(2,1)S(1)} collective-permute-done((bf16[2,400,384]{2,1,0:T(8,128)(2,1)S(1)}, bf16[2,400,384]{2,1,0:T(8,128)(2,1)S(1)}, u32[]{:S(2)}, u32[]{:S(2)}) %collective-permute-start.11) | collective-permute-done | bytes 614432 | tf_op jit(solution)/shard_map/ppermute | solution.py:268
  96.5 2.7 %collective-permute-start.21 = (bf16[2,2,96,384]{3,2,1,0:T(8,128)(2,1)S(1)}, bf16[2,2,96,384]{3,2,1,0:T(8,128)(2,1)S(1)}, u32[]{:S(2)}, u32[]{:S(2)}) collective-permute-start(bf16[2,2,96,384]{3,2,1,0:T(8,128)(2,1)S(1)} %get-tuple-element.62), channel_id=1, source_target_pairs={{0,8},{8,16},{16,24},{24,0},{32,40},{40,48},{48,56},{56,32},{64,72... | collective-permute-start | bytes 884744 | tf_op jit(solution)/shard_map/ppermute | solution.py:268
  99.2 0.5 fusion.7
  99.7 0.1 collective-permute-start.20
  99.8 3.7 %collective-permute-done.23 = bf16[2,2,96,384]{3,2,1,0:T(8,128)(2,1)S(1)} collective-permute-done((bf16[2,2,96,384]{3,2,1,0:T(8,128)(2,1)S(1)}, bf16[2,2,96,384]{3,2,1,0:T(8,128)(2,1)S(1)}, u32[]{:S(2)}, u32[]{:S(2)}) %collective-permute-start.23) | collective-permute-done | bytes 294944 | tf_op jit(solution)/shard_map/ppermute | solution.py:268
  103.6 2.7 %collective-permute-start.18 = (bf16[2,400,384]{2,1,0:T(8,128)(2,1)S(1)}, bf16[2,400,384]{2,1,0:T(8,128)(2,1)S(1)}, u32[]{:S(2)}, u32[]{:S(2)}) collective-permute-start(bf16[2,400,384]{2,1,0:T(8,128)(2,1)S(1)} %get-tuple-element.66), channel_id=1, source_target_pairs={{0,2},{1,7},{2,4},{3,1},{4,6},{5,3},{6,0},{7,5},{8,10},{9,15},{10,... | collective-permute-start | bytes 1843208 | tf_op jit(solution)/shard_map/ppermute | solution.py:273
  106.3 3.4 %collective-permute-start.16 = (bf16[4,400,384]{2,1,0:T(8,128)(2,1)S(1)}, bf16[4,400,384]{2,1,0:T(8,128)(2,1)S(1)}, u32[]{:S(2)}, u32[]{:S(2)}) collective-permute-start(bf16[4,400,384]{2,1,0:T(8,128)(2,1)S(1)} %get-tuple-element.58.rest_5_), channel_id=1, source_target_pairs={{0,1},{1,0},{2,3},{3,2},{4,5},{5,4},{6,7},{7,6},{8,9},{9,8},{10,11... | collective-permute-start | bytes 3686408 | tf_op jit(solution)/shard_map/ppermute | solution.py:277
  109.7 0.2 fusion.18
  109.9 0.1 collective-permute-start.25
  110.0 0.6 fusion.13
  110.5 2.4 %collective-permute-done.20 = bf16[2,400,384]{2,1,0:T(8,128)(2,1)S(1)} collective-permute-done((bf16[2,400,384]{2,1,0:T(8,128)(2,1)S(1)}, bf16[2,400,384]{2,1,0:T(8,128)(2,1)S(1)}, u32[]{:S(2)}, u32[]{:S(2)}) %collective-permute-start.20) | collective-permute-done | bytes 614432 | tf_op jit(solution)/shard_map/ppermute | solution.py:273
  113.0 1.0 collective-permute-start.26
  113.9 16.3 %collective-permute-done.19 = bf16[2,400,384]{2,1,0:T(8,128)(2,1)S(1)} collective-permute-done((bf16[2,400,384]{2,1,0:T(8,128)(2,1)S(1)}, bf16[2,400,384]{2,1,0:T(8,128)(2,1)S(1)}, u32[]{:S(2)}, u32[]{:S(2)}) %collective-permute-start.19) | collective-permute-done | bytes 614432 | tf_op jit(solution)/shard_map/ppermute | solution.py:273
  130.3 1.9 %collective-permute-start.28 = (bf16[2,304,384]{2,1,0:T(8,128)(2,1)S(1)}, bf16[2,304,384]{2,1,0:T(8,128)(2,1)S(1)}, u32[]{:S(2)}, u32[]{:S(2)}) collective-permute-start(bf16[2,304,384]{2,1,0:T(8,128)(2,1)S(1)} %get-tuple-element.70), channel_id=1, source_target_pairs={{0,16},{8,24},{16,0},{24,8},{32,48},{40,56},{48,32},{56,40},{64,80... | collective-permute-start | bytes 1400840 | tf_op jit(solution)/shard_map/ppermute | solution.py:268
  132.2 0.4 fusion.5
  132.6 0.2 slice_add_fusion
  132.8 0.1 collective-permute-start.24
  132.9 2.7 %collective-permute-start.22 = (bf16[2,96,384]{2,1,0:T(8,128)(2,1)S(1)}, bf16[2,96,384]{2,1,0:T(8,128)(2,1)S(1)}, u32[]{:S(2)}, u32[]{:S(2)}) collective-permute-start(bf16[2,96,384]{2,1,0:T(8,128)(2,1)S(1)} %get-tuple-element.74), channel_id=1, source_target_pairs={{0,32},{8,40},{16,48},{24,56},{32,64},{40,72},{48,80},{56,88},{64,... | collective-permute-start | bytes 442376 | tf_op jit(solution)/shard_map/ppermute | solution.py:268
  135.5 9.2 %shard_map.60 = bf16[8,2,400,400]{3,2,1,0:T(8,128)(2,1)} custom-call(s32[8]{0:T(128)S(1)} %copy-done.1, bf16[8,2,400,384]{3,2,1,0:T(8,128)(2,1)} %get-tuple-element.41.left_hbm, bf16[4,400,384]{2,1,0:T(8,128)(2,1)} %copy-done.3, bf16[4,400,384]{2,1,0:T(8,128)(2,1)} %copy-done.5, bf16[4,400,384]{2,1,0:T(8,128)(2,1)} %copy-done.6, ...), custom_call_target="tpu_custom_call" | custom-call | flops 1966080000 | bytes 15000000 | tf_op jit(solution)/shard_map/pallas_call | solution.py:218
  144.8 0.1 slice_add_fusion.1.bottom_ref
  144.9 4.0 %collective-permute-done.27.rest_1_ = bf16[2,304,384]{2,1,0:T(8,128)(2,1)S(1)} collective-permute-done((bf16[2,304,384]{2,1,0:T(8,128)(2,1)S(1)}, bf16[2,304,384]{2,1,0:T(8,128)(2,1)S(1)}, u32[]{:S(2)}, u32[]{:S(2)}) %collective-permute-start.27) | collective-permute-done | bytes 466976 | tf_op jit(solution)/shard_map/ppermute | solution.py:268
  148.9 2.1 %shard_map.61 = f32[2,400,400]{2,1,0:T(8,128)} custom-call(bf16[400,384]{1,0:T(8,128)(2,1)S(1)} %bitcast.51, f32[2,304,384]{2,1,0:T(8,128)S(1)} %slice_add_fusion, f32[2,96,384]{2,1,0:T(8,128)S(1)} %slice_add_fusion.1.bottom_ref, bf16[2,304,384]{2,1,0:T(8,128)(2,1)S(1)} %collective-permute-done.26.rest_0_, ...), custom_call_target="tpu_custom_call" | custom-call | tf_op jit(solution)/shard_map/pallas_call | solution.py:254
  (63 shorter events, 0.3 us)
Async XLA Ops:
  0.6 32.2 %copy-start = (bf16[1,384,400]{1,2,0:T(8,128)(2,1)S(1)}, bf16[1,384,400]{1,2,0:T(8,128)(2,1)}, u32[]{:S(2)}) copy-start(bf16[1,384,400]{1,2,0:T(8,128)(2,1)} %param.4) | copy-start | bytes 921604
  0.6 8.4 %collective-permute-start.2 = (bf16[400,384]{1,0:T(8,128)(2,1)}, bf16[400,384]{1,0:T(8,128)(2,1)S(1)}, u32[]{:S(2)}, u32[]{:S(2)}) collective-permute-start(bf16[400,384]{1,0:T(8,128)(2,1)} %bitcast.43), channel_id=1, source_target_pairs={{0,32},{8,40},{16,48},{24,56},{32,64},{40,72},{48,80},{56,88},{64,... | collective-permute-start | bytes 921608 | tf_op jit(solution)/shard_map/ppermute | solution.py:268
  0.9 31.9 %collective-permute-start.1 = (bf16[400,384]{1,0:T(8,128)(2,1)}, bf16[400,384]{1,0:T(8,128)(2,1)S(1)}, u32[]{:S(2)}, u32[]{:S(2)}) collective-permute-start(bf16[400,384]{1,0:T(8,128)(2,1)} %bitcast.44), channel_id=1, source_target_pairs={{0,64},{8,72},{16,80},{24,88},{32,96},{40,104},{48,112},{56,120},{... | collective-permute-start | bytes 921608 | tf_op jit(solution)/shard_map/ppermute | solution.py:268
  3.0 29.7 %collective-permute-start = (bf16[400,384]{1,0:T(8,128)(2,1)}, bf16[400,384]{1,0:T(8,128)(2,1)S(1)}, u32[]{:S(2)}, u32[]{:S(2)}) collective-permute-start(bf16[400,384]{1,0:T(8,128)(2,1)} %bitcast.45), channel_id=1, source_target_pairs={{0,96},{8,104},{16,112},{24,120},{32,0},{40,8},{48,16},{56,24},{64... | collective-permute-start | bytes 921608 | tf_op jit(solution)/shard_map/ppermute | solution.py:268
  3.1 29.7 %collective-permute-start.15 = (bf16[400,384]{1,0:T(8,128)(2,1)}, bf16[400,384]{1,0:T(8,128)(2,1)S(1)}, u32[]{:S(2)}, u32[]{:S(2)}) collective-permute-start(bf16[400,384]{1,0:T(8,128)(2,1)} %bitcast.46), channel_id=1, source_target_pairs={{0,4},{1,5},{2,6},{3,7},{4,0},{5,1},{6,2},{7,3},{8,12},{9,13},{10,... | collective-permute-start | bytes 921608 | tf_op jit(solution)/shard_map/ppermute | solution.py:273
  6.6 26.2 %collective-permute-start.14 = (bf16[400,384]{1,0:T(8,128)(2,1)}, bf16[400,384]{1,0:T(8,128)(2,1)S(1)}, u32[]{:S(2)}, u32[]{:S(2)}) collective-permute-start(bf16[400,384]{1,0:T(8,128)(2,1)} %bitcast.47), channel_id=1, source_target_pairs={{0,6},{1,3},{2,0},{3,5},{4,2},{5,7},{6,4},{7,1},{8,14},{9,11},{10,... | collective-permute-start | bytes 921608 | tf_op jit(solution)/shard_map/ppermute | solution.py:273
  9.1 23.8 %collective-permute-start.13 = (bf16[400,384]{1,0:T(8,128)(2,1)}, bf16[400,384]{1,0:T(8,128)(2,1)S(1)}, u32[]{:S(2)}, u32[]{:S(2)}) collective-permute-start(bf16[400,384]{1,0:T(8,128)(2,1)} %bitcast.48), channel_id=1, source_target_pairs={{0,2},{1,7},{2,4},{3,1},{4,6},{5,3},{6,0},{7,5},{8,10},{9,15},{10,... | collective-permute-start | bytes 921608 | tf_op jit(solution)/shard_map/ppermute | solution.py:273
  12.8 0.7 copy-start.1
  13.5 0.7 copy-start.2
  32.8 4.7 %copy-start.18 = (bf16[4,2,304,384]{3,2,1,0:T(8,128)(2,1)S(1)}, bf16[4,2,304,384]{3,2,1,0:T(8,128)(2,1)}, u32[]{:S(2)}) copy-start(bf16[4,2,304,384]{3,2,1,0:T(8,128)(2,1)} %get-tuple-element.36) | copy-start | bytes 5603332
  32.8 4.7 %copy-start.17 = (bf16[4,2,400,384]{3,2,1,0:T(8,128)(2,1)S(1)}, bf16[4,2,400,384]{3,2,1,0:T(8,128)(2,1)}, u32[]{:S(2)}) copy-start(bf16[4,2,400,384]{3,2,1,0:T(8,128)(2,1)} %get-tuple-element.60) | copy-start | bytes 7372804
  33.2 49.0 %copy-start.3 = (bf16[4,400,384]{2,1,0:T(8,128)(2,1)}, bf16[4,400,384]{2,1,0:T(8,128)(2,1)S(1)}, u32[]{:S(2)}) copy-start(bf16[4,400,384]{2,1,0:T(8,128)(2,1)S(1)} %get-tuple-element.42.rest_0_) | copy-start | bytes 3686404
  33.2 73.0 %copy-start.4 = (bf16[4,400,384]{2,1,0:T(8,128)(2,1)}, bf16[4,400,384]{2,1,0:T(8,128)(2,1)S(1)}, u32[]{:S(2)}) copy-start(bf16[4,400,384]{2,1,0:T(8,128)(2,1)S(1)} %get-tuple-element.58.rest_5_) | copy-start | bytes 3686404
  33.3 51.7 %collective-permute-start.4 = (bf16[4,2,304,384]{3,2,1,0:T(8,128)(2,1)}, bf16[4,2,304,384]{3,2,1,0:T(8,128)(2,1)S(1)}, u32[]{:S(2)}, u32[]{:S(2)}) collective-permute-start(bf16[4,2,304,384]{3,2,1,0:T(8,128)(2,1)} %get-tuple-element.38), channel_id=1, source_target_pairs={{0,32},{8,40},{16,48},{24,56},{32,64},{40,72},{48,80},{56,88},{64,... | collective-permute-start | bytes 5603336 | tf_op jit(solution)/shard_map/ppermute | solution.py:268
  34.9 29.9 %collective-permute-start.7 = (bf16[4,400,384]{2,1,0:T(8,128)(2,1)S(1)}, bf16[4,400,384]{2,1,0:T(8,128)(2,1)S(1)}, u32[]{:S(2)}, u32[]{:S(2)}) collective-permute-start(bf16[4,400,384]{2,1,0:T(8,128)(2,1)S(1)} %get-tuple-element.42.rest_0_), channel_id=1, source_target_pairs={{0,24},{8,0},{16,8},{24,16},{32,56},{40,32},{48,40},{56,48},{64,88... | collective-permute-start | bytes 3686408 | tf_op jit(solution)/shard_map/ppermute | solution.py:268
  35.4 29.4 %collective-permute-start.8 = (bf16[4,400,384]{2,1,0:T(8,128)(2,1)S(1)}, bf16[4,400,384]{2,1,0:T(8,128)(2,1)S(1)}, u32[]{:S(2)}, u32[]{:S(2)}) collective-permute-start(bf16[4,400,384]{2,1,0:T(8,128)(2,1)S(1)} %get-tuple-element.42.rest_0_), channel_id=1, source_target_pairs={{0,8},{8,16},{16,24},{24,0},{32,40},{40,48},{48,56},{56,32},{64,72... | collective-permute-start | bytes 3686408 | tf_op jit(solution)/shard_map/ppermute | solution.py:268
  37.6 47.8 %collective-permute-start.3 = (bf16[4,2,304,384]{3,2,1,0:T(8,128)(2,1)S(1)}, bf16[4,2,304,384]{3,2,1,0:T(8,128)(2,1)S(1)}, u32[]{:S(2)}, u32[]{:S(2)}) collective-permute-start(bf16[4,2,304,384]{3,2,1,0:T(8,128)(2,1)S(1)} %copy-done.18), channel_id=1, source_target_pairs={{0,96},{8,104},{16,112},{24,120},{32,0},{40,8},{48,16},{56,24},{64... | collective-permute-start | bytes 5603336 | tf_op jit(solution)/shard_map/ppermute | solution.py:268
  37.6 61.6 %collective-permute-start.17 = (bf16[4,2,400,384]{3,2,1,0:T(8,128)(2,1)S(1)}, bf16[4,2,400,384]{3,2,1,0:T(8,128)(2,1)S(1)}, u32[]{:S(2)}, u32[]{:S(2)}) collective-permute-start(bf16[4,2,400,384]{3,2,1,0:T(8,128)(2,1)S(1)} %copy-done.17), channel_id=1, source_target_pairs={{0,1},{1,0},{2,3},{3,2},{4,5},{5,4},{6,7},{7,6},{8,9},{9,8},{10,11... | collective-permute-start | bytes 7372808 | tf_op jit(solution)/shard_map/ppermute | solution.py:277
  64.8 21.6 %copy-start.5 = (bf16[4,400,384]{2,1,0:T(8,128)(2,1)}, bf16[4,400,384]{2,1,0:T(8,128)(2,1)S(1)}, u32[]{:S(2)}) copy-start(bf16[4,400,384]{2,1,0:T(8,128)(2,1)S(1)} %collective-permute-done.7.rest_1_) | copy-start | bytes 3686404
  64.8 21.7 %copy-start.6 = (bf16[4,400,384]{2,1,0:T(8,128)(2,1)}, bf16[4,400,384]{2,1,0:T(8,128)(2,1)S(1)}, u32[]{:S(2)}) copy-start(bf16[4,400,384]{2,1,0:T(8,128)(2,1)S(1)} %collective-permute-done.8.rest_2_) | copy-start | bytes 3686404
  64.8 20.2 %copy-start.11 = (bf16[2,2,304,384]{3,2,1,0:T(8,128)(2,1)S(1)}, bf16[2,2,304,384]{3,2,1,0:T(8,128)(2,1)}, u32[]{:S(2)}) copy-start(bf16[2,2,304,384]{3,2,1,0:T(8,128)(2,1)} %get-tuple-element.37) | copy-start | bytes 2801668
  64.8 14.4 %collective-permute-start.9 = (bf16[4,2,96,384]{3,2,1,0:T(8,128)(2,1)}, bf16[4,2,96,384]{3,2,1,0:T(8,128)(2,1)S(1)}, u32[]{:S(2)}, u32[]{:S(2)}) collective-permute-start(bf16[4,2,96,384]{3,2,1,0:T(8,128)(2,1)} %get-tuple-element.47), channel_id=1, source_target_pairs={{0,8},{8,16},{16,24},{24,0},{32,40},{40,48},{48,56},{56,32},{64,72... | collective-permute-start | bytes 1769480 | tf_op jit(solution)/shard_map/ppermute | solution.py:268
  67.1 14.9 %collective-permute-start.10 = (bf16[4,2,96,384]{3,2,1,0:T(8,128)(2,1)}, bf16[4,2,96,384]{3,2,1,0:T(8,128)(2,1)S(1)}, u32[]{:S(2)}, u32[]{:S(2)}) collective-permute-start(bf16[4,2,96,384]{3,2,1,0:T(8,128)(2,1)} %get-tuple-element.48), channel_id=1, source_target_pairs={{0,24},{8,0},{16,8},{24,16},{32,56},{40,32},{48,40},{56,48},{64,88... | collective-permute-start | bytes 1769480 | tf_op jit(solution)/shard_map/ppermute | solution.py:268
  82.1 14.3 %collective-permute-start.11 = (bf16[2,400,384]{2,1,0:T(8,128)(2,1)S(1)}, bf16[2,400,384]{2,1,0:T(8,128)(2,1)S(1)}, u32[]{:S(2)}, u32[]{:S(2)}) collective-permute-start(bf16[2,400,384]{2,1,0:T(8,128)(2,1)S(1)} %slice.136), channel_id=1, source_target_pairs={{0,24},{8,0},{16,8},{24,16},{32,56},{40,32},{48,40},{56,48},{64,88... | collective-permute-start | bytes 1843208 | tf_op jit(solution)/shard_map/ppermute | solution.py:268
  82.2 14.2 %collective-permute-start.12 = (bf16[2,400,384]{2,1,0:T(8,128)(2,1)S(1)}, bf16[2,400,384]{2,1,0:T(8,128)(2,1)S(1)}, u32[]{:S(2)}, u32[]{:S(2)}) collective-permute-start(bf16[2,400,384]{2,1,0:T(8,128)(2,1)S(1)} %slice.137), channel_id=1, source_target_pairs={{0,8},{8,16},{16,24},{24,0},{32,40},{40,48},{48,56},{56,32},{64,72... | collective-permute-start | bytes 1843208 | tf_op jit(solution)/shard_map/ppermute | solution.py:268
  85.0 1.2 copy-start.10
  85.0 2.2 %copy-start.16 = (bf16[2,2,96,384]{3,2,1,0:T(8,128)(2,1)S(1)}, bf16[2,2,96,384]{3,2,1,0:T(8,128)(2,1)}, u32[]{:S(2)}) copy-start(bf16[2,2,96,384]{3,2,1,0:T(8,128)(2,1)} %get-tuple-element.53) | copy-start | bytes 884740
  85.2 21.0 %collective-permute-start.5 = (bf16[2,2,304,384]{3,2,1,0:T(8,128)(2,1)S(1)}, bf16[2,2,304,384]{3,2,1,0:T(8,128)(2,1)S(1)}, u32[]{:S(2)}, u32[]{:S(2)}) collective-permute-start(bf16[2,2,304,384]{3,2,1,0:T(8,128)(2,1)S(1)} %add_convert_fusion.1), channel_id=1, source_target_pairs={{0,32},{8,40},{16,48},{24,56},{32,64},{40,72},{48,80},{56,88},{64,... | collective-permute-start | bytes 2801672 | tf_op jit(solution)/shard_map/ppermute | solution.py:268
  86.2 1.0 copy-start.15
  86.2 13.0 %copy-start.7 = (bf16[4,2,400,384]{3,2,1,0:T(8,128)(2,1)S(1)}, bf16[4,2,400,384]{3,2,1,0:T(8,128)(2,1)}, u32[]{:S(2)}) copy-start(bf16[4,2,400,384]{3,2,1,0:T(8,128)(2,1)} %get-tuple-element.59) | copy-start | bytes 7372804
  86.4 23.4 %collective-permute-start.6 = (bf16[2,2,304,384]{3,2,1,0:T(8,128)(2,1)S(1)}, bf16[2,2,304,384]{3,2,1,0:T(8,128)(2,1)S(1)}, u32[]{:S(2)}, u32[]{:S(2)}) collective-permute-start(bf16[2,2,304,384]{3,2,1,0:T(8,128)(2,1)S(1)} %add_convert_fusion), channel_id=1, source_target_pairs={{0,96},{8,104},{16,112},{24,120},{32,0},{40,8},{48,16},{56,24},{64... | collective-permute-start | bytes 2801672 | tf_op jit(solution)/shard_map/ppermute | solution.py:268
  96.4 3.3 %copy-start.12 = (bf16[2,400,384]{2,1,0:T(8,128)(2,1)}, bf16[2,400,384]{2,1,0:T(8,128)(2,1)S(1)}, u32[]{:S(2)}) copy-start(bf16[2,400,384]{2,1,0:T(8,128)(2,1)S(1)} %collective-permute-done.11.rest_3_) | copy-start | bytes 1843204
  96.4 3.3 %copy-start.13 = (bf16[2,400,384]{2,1,0:T(8,128)(2,1)}, bf16[2,400,384]{2,1,0:T(8,128)(2,1)S(1)}, u32[]{:S(2)}) copy-start(bf16[2,400,384]{2,1,0:T(8,128)(2,1)S(1)} %collective-permute-done.12.rest_4_) | copy-start | bytes 1843204
  96.4 7.1 %collective-permute-start.23 = (bf16[2,2,96,384]{3,2,1,0:T(8,128)(2,1)S(1)}, bf16[2,2,96,384]{3,2,1,0:T(8,128)(2,1)S(1)}, u32[]{:S(2)}, u32[]{:S(2)}) collective-permute-start(bf16[2,2,96,384]{3,2,1,0:T(8,128)(2,1)S(1)} %get-tuple-element.63), channel_id=1, source_target_pairs={{0,24},{8,0},{16,8},{24,16},{32,56},{40,32},{48,40},{56,48},{64,88... | collective-permute-start | bytes 884744 | tf_op jit(solution)/shard_map/ppermute | solution.py:268
  96.5 7.1 %collective-permute-start.21 = (bf16[2,2,96,384]{3,2,1,0:T(8,128)(2,1)S(1)}, bf16[2,2,96,384]{3,2,1,0:T(8,128)(2,1)S(1)}, u32[]{:S(2)}, u32[]{:S(2)}) collective-permute-start(bf16[2,2,96,384]{3,2,1,0:T(8,128)(2,1)S(1)} %get-tuple-element.62), channel_id=1, source_target_pairs={{0,8},{8,16},{16,24},{24,0},{32,40},{40,48},{48,56},{56,32},{64,72... | collective-permute-start | bytes 884744 | tf_op jit(solution)/shard_map/ppermute | solution.py:268
  99.2 10.5 %copy-start.14 = (bf16[4,2,96,384]{3,2,1,0:T(8,128)(2,1)S(1)}, bf16[4,2,96,384]{3,2,1,0:T(8,128)(2,1)}, u32[]{:S(2)}) copy-start(bf16[4,2,96,384]{3,2,1,0:T(8,128)(2,1)} %get-tuple-element.61) | copy-start | bytes 1769476
  99.2 10.8 %copy-start.8 = (bf16[4,2,304,384]{3,2,1,0:T(8,128)(2,1)S(1)}, bf16[4,2,304,384]{3,2,1,0:T(8,128)(2,1)}, u32[]{:S(2)}) copy-start(bf16[4,2,304,384]{3,2,1,0:T(8,128)(2,1)} %get-tuple-element.33) | copy-start | bytes 5603332
  99.7 13.2 %collective-permute-start.20 = (bf16[2,400,384]{2,1,0:T(8,128)(2,1)S(1)}, bf16[2,400,384]{2,1,0:T(8,128)(2,1)S(1)}, u32[]{:S(2)}, u32[]{:S(2)}) collective-permute-start(bf16[2,400,384]{2,1,0:T(8,128)(2,1)S(1)} %get-tuple-element.67), channel_id=1, source_target_pairs={{0,4},{1,5},{2,6},{3,7},{4,0},{5,1},{6,2},{7,3},{8,12},{9,13},{10,... | collective-permute-start | bytes 1843208 | tf_op jit(solution)/shard_map/ppermute | solution.py:273
  103.6 26.7 %collective-permute-start.19 = (bf16[2,400,384]{2,1,0:T(8,128)(2,1)S(1)}, bf16[2,400,384]{2,1,0:T(8,128)(2,1)S(1)}, u32[]{:S(2)}, u32[]{:S(2)}) collective-permute-start(bf16[2,400,384]{2,1,0:T(8,128)(2,1)S(1)} %get-tuple-element.68), channel_id=1, source_target_pairs={{0,6},{1,3},{2,0},{3,5},{4,2},{5,7},{6,4},{7,1},{8,14},{9,11},{10,... | collective-permute-start | bytes 1843208 | tf_op jit(solution)/shard_map/ppermute | solution.py:273
  103.6 26.7 %collective-permute-start.18 = (bf16[2,400,384]{2,1,0:T(8,128)(2,1)S(1)}, bf16[2,400,384]{2,1,0:T(8,128)(2,1)S(1)}, u32[]{:S(2)}, u32[]{:S(2)}) collective-permute-start(bf16[2,400,384]{2,1,0:T(8,128)(2,1)S(1)} %get-tuple-element.66), channel_id=1, source_target_pairs={{0,2},{1,7},{2,4},{3,1},{4,6},{5,3},{6,0},{7,5},{8,10},{9,15},{10,... | collective-permute-start | bytes 1843208 | tf_op jit(solution)/shard_map/ppermute | solution.py:273
  106.3 26.5 %collective-permute-start.16 = (bf16[4,400,384]{2,1,0:T(8,128)(2,1)S(1)}, bf16[4,400,384]{2,1,0:T(8,128)(2,1)S(1)}, u32[]{:S(2)}, u32[]{:S(2)}) collective-permute-start(bf16[4,400,384]{2,1,0:T(8,128)(2,1)S(1)} %get-tuple-element.58.rest_5_), channel_id=1, source_target_pairs={{0,1},{1,0},{2,3},{3,2},{4,5},{5,4},{6,7},{7,6},{8,9},{9,8},{10,11... | collective-permute-start | bytes 3686408 | tf_op jit(solution)/shard_map/ppermute | solution.py:277
  109.9 23.0 %collective-permute-start.25 = (bf16[2,96,384]{2,1,0:T(8,128)(2,1)S(1)}, bf16[2,96,384]{2,1,0:T(8,128)(2,1)S(1)}, u32[]{:S(2)}, u32[]{:S(2)}) collective-permute-start(bf16[2,96,384]{2,1,0:T(8,128)(2,1)S(1)} %get-tuple-element.73), channel_id=1, source_target_pairs={{0,64},{8,72},{16,80},{24,88},{32,96},{40,104},{48,112},{56,120},{... | collective-permute-start | bytes 442376 | tf_op jit(solution)/shard_map/ppermute | solution.py:268
  113.0 32.0 %collective-permute-start.26 = (bf16[2,304,384]{2,1,0:T(8,128)(2,1)S(1)}, bf16[2,304,384]{2,1,0:T(8,128)(2,1)S(1)}, u32[]{:S(2)}, u32[]{:S(2)}) collective-permute-start(bf16[2,304,384]{2,1,0:T(8,128)(2,1)S(1)} %get-tuple-element.71), channel_id=1, source_target_pairs={{0,8},{8,16},{16,24},{24,0},{32,40},{40,48},{48,56},{56,32},{64,72... | collective-permute-start | bytes 1400840 | tf_op jit(solution)/shard_map/ppermute | solution.py:268
  130.3 18.6 %collective-permute-start.27 = (bf16[2,304,384]{2,1,0:T(8,128)(2,1)S(1)}, bf16[2,304,384]{2,1,0:T(8,128)(2,1)S(1)}, u32[]{:S(2)}, u32[]{:S(2)}) collective-permute-start(bf16[2,304,384]{2,1,0:T(8,128)(2,1)S(1)} %get-tuple-element.69), channel_id=1, source_target_pairs={{0,24},{8,0},{16,8},{24,16},{32,56},{40,32},{48,40},{56,48},{64,88... | collective-permute-start | bytes 1400840 | tf_op jit(solution)/shard_map/ppermute | solution.py:268
  130.3 18.6 %collective-permute-start.28 = (bf16[2,304,384]{2,1,0:T(8,128)(2,1)S(1)}, bf16[2,304,384]{2,1,0:T(8,128)(2,1)S(1)}, u32[]{:S(2)}, u32[]{:S(2)}) collective-permute-start(bf16[2,304,384]{2,1,0:T(8,128)(2,1)S(1)} %get-tuple-element.70), channel_id=1, source_target_pairs={{0,16},{8,24},{16,0},{24,8},{32,48},{40,56},{48,32},{56,40},{64,80... | collective-permute-start | bytes 1400840 | tf_op jit(solution)/shard_map/ppermute | solution.py:268
  132.8 2.8 %copy-start.9 = (bf16[4,400,384]{2,1,0:T(8,128)(2,1)}, bf16[4,400,384]{2,1,0:T(8,128)(2,1)S(1)}, u32[]{:S(2)}) copy-start(bf16[4,400,384]{2,1,0:T(8,128)(2,1)S(1)} %collective-permute-done.16.rest_6_) | copy-start | bytes 3686404
  132.8 12.0 %collective-permute-start.24 = (bf16[2,96,384]{2,1,0:T(8,128)(2,1)S(1)}, bf16[2,96,384]{2,1,0:T(8,128)(2,1)S(1)}, u32[]{:S(2)}, u32[]{:S(2)}) collective-permute-start(bf16[2,96,384]{2,1,0:T(8,128)(2,1)S(1)} %get-tuple-element.72), channel_id=1, source_target_pairs={{0,96},{8,104},{16,112},{24,120},{32,0},{40,8},{48,16},{56,24},{64... | collective-permute-start | bytes 442376 | tf_op jit(solution)/shard_map/ppermute | solution.py:268
  132.9 11.9 %collective-permute-start.22 = (bf16[2,96,384]{2,1,0:T(8,128)(2,1)S(1)}, bf16[2,96,384]{2,1,0:T(8,128)(2,1)S(1)}, u32[]{:S(2)}, u32[]{:S(2)}) collective-permute-start(bf16[2,96,384]{2,1,0:T(8,128)(2,1)S(1)} %get-tuple-element.74), channel_id=1, source_target_pairs={{0,32},{8,40},{16,48},{24,56},{32,64},{40,72},{48,80},{56,88},{64,... | collective-permute-start | bytes 442376 | tf_op jit(solution)/shard_map/ppermute | solution.py:268
